TPU v7x, 32 devices: a whole 2x2x4 slice. The times are simulated.
32 devices in a mesh: dp: 8 (over y, x, core), freq: 4 (over z).
Axes of the slice: x: 2, y: 2, z: 4, core: 2. Of those that a mesh axis runs over, the one named last changes fastest.
Arguments:
- inputs: float32 [512, 16, 768], P('freq', 'dp'), may hold values from -6 to 6
- cotangent: float32 [512, 16, 768], P('freq', 'dp'), may hold values from -6 to 6
- group: int32 [16], P('dp'), may hold values from 0 to 1, as said below
- lens: int32 [16, 4], P('dp'), may hold values from 64 to 128, as said below
- norm1_gain: float32 [768], replicated, may hold values from 0.25 to 1.75
- w_in: bfloat16 [768, 2304], P('freq'), may hold values from -0.21875 to 0.21875
- kernel_long: bfloat16 [512, 768], P('freq'), may hold values from -4 to 4
- kernel_short: bfloat16 [128, 768], P('freq'), may hold values from -4 to 4
- conv_weight: float32 [3, 768], replicated, may hold values from -2.5 to 2.5
- cond_gain: float32 [768], replicated, may hold values from 0.5 to 2
- w_out: bfloat16 [768, 768], P('freq'), may hold values from -0.21875 to 0.21875
- norm2_gain: float32 [768], replicated, may hold values from 0.25 to 1.75
- w_gate_up: bfloat16 [768, 6144], P('freq'), may hold values from -0.21875 to 0.21875
- w_down: bfloat16 [3072, 768], P('freq'), may hold values from -0.109375 to 0.109375
Outputs:
- layer_out: float32 [512, 16, 768], P('freq', 'dp')
- grad_inputs: float32 [512, 16, 768], P('freq', 'dp')
- grad_norm1_gain: float32 [768], replicated
- grad_w_in: float32 [768, 2304], P('freq')
- grad_kernel_long: float32 [512, 768], replicated
- grad_kernel_short: float32 [128, 768], replicated
- grad_conv_weight: float32 [3, 768], replicated
- grad_cond_gain: float32 [768], replicated
- grad_w_out: float32 [768, 768], P('freq')
- grad_norm2_gain: float32 [768], replicated
- grad_w_gate_up: float32 [768, 6144], P('freq')
- grad_w_down: float32 [3072, 768], P('freq')
Inputs may be any that keep to these rules, and one draw needn't show every extreme that they name: Some slot has group 0 and some slot has group 1. `lens`: a group 0 slot holds one sequence whose length is the sum of its four counts; a group 1 slot holds four sequences with these lengths; some group 0 slot has all four counts equal to 128.
All inputs are finite; a program needn't handle non-finite values.
Results may differ from a plain program's by a relative error of at most 0.024.
Values may be sent and summed in bfloat16 or wider, within the bound.
No kernel may reach another device: no remote copies, remote signals or barrier semaphores. Data moves between devices by JAX's collectives and lax.ppermute only.
A program may use at most 192 MiB of HBM per device.

v0:
```python
import math

import jax
import jax.numpy as jnp
import numpy as np
from jax import lax
from jax.experimental import pallas as pl
from jax.experimental.pallas import tpu as pltpu
from jax.sharding import PartitionSpec as P

SHORT_LENGTH = 128
EPSILON = 1e-05
BF = jnp.bfloat16
F32 = jnp.float32
GROUP = 8
RIDE = 16
GELU_A = math.sqrt(2.0 / math.pi)
GELU_B = 0.044715


def cosine_table(length):
    freq = np.arange(length)[:, None]
    posit = np.arange(length)[None, :]
    phase = (2 * posit + 1) * freq % (4 * length)
    weight = np.where(freq == 0, 1.0, 2.0) / length
    return (np.cos(phase * (math.pi / (2 * length))) * np.sqrt(weight)).astype(np.float32)


def dot(a, b):
    return lax.dot_general(a, b, (((1,), (0,)), ((), ())), preferred_element_type=F32)


def dot_nt(a, b):
    return lax.dot_general(a, b, (((1,), (1,)), ((), ())), preferred_element_type=F32)


def dot_tn(a, b):
    return lax.dot_general(a, b, (((0,), (0,)), ((), ())), preferred_element_type=F32)


def norm_parts(values):
    center = values - jnp.mean(values, axis=-1, keepdims=True)
    spread = jnp.mean(center * center, axis=-1, keepdims=True)
    inv = lax.rsqrt(spread + EPSILON)
    return center * inv, inv


def norm_pull(hat, inv, gain, grad):
    scaled = grad * gain
    mean_one = jnp.mean(scaled, axis=-1, keepdims=True)
    mean_two = jnp.mean(scaled * hat, axis=-1, keepdims=True)
    return inv * (scaled - mean_one - hat * mean_two), jnp.sum(grad * hat, axis=0, keepdims=True)


def pick(stacked, index):
    return lax.dynamic_index_in_dim(stacked, index, axis=0, keepdims=False)


def run(kernel, name, outs, where, ins, scratch=(), after=(), flops=0):
    n_in, n_after = len(ins), len(after)

    def wrapped(*refs):
        kernel(*refs[: 1 + n_in], *refs[1 + n_in + n_after :])

    size = sum(x.size * x.dtype.itemsize for x in ins)
    size += sum(math.prod(s) * jnp.dtype(t).itemsize for s, t in outs)
    return pl.pallas_call(
        wrapped,
        out_shape=[jax.ShapeDtypeStruct(s, t) for s, t in outs],
        in_specs=[pl.BlockSpec(memory_space=pltpu.SMEM)]
        + [pl.BlockSpec(memory_space=pltpu.VMEM)] * n_in
        + [pl.BlockSpec(memory_space=pl.ANY)] * n_after,
        out_specs=[pl.BlockSpec(memory_space=pltpu.VMEM)] * len(outs),
        scratch_shapes=list(scratch),
        compiler_params=pltpu.CompilerParams(vmem_limit_bytes=50 * 2**20),
        cost_estimate=pl.CostEstimate(flops=int(flops), bytes_accessed=int(size), transcendentals=0),
        name=name,
    )(where, *ins, *after)


def rows_at(index, size):
    return pl.ds(pl.multiple_of(index * size, 16), size)


def project_kernel(where, na, nb, local, n1, n2, n3, c1, c2, c3, mask, w, outer, left, right, v0, v1, v2, v3, vals):
    z, chip = where[0], where[1]
    rows = local.shape[0]
    quarter = rows // 4
    half = outer.shape[1]
    w[rows_at(z, rows), :] = local[...]
    for k, near in ((1, n1), (2, n2), (3, n3)):
        base = ((z - k) & 3) * 4
        w[rows_at(base + chip, quarter), :] = near[...]
        for m, far in ((1, c1), (2, c2), (3, c3)):
            w[rows_at(base + (chip ^ m), quarter), :] = far[k - 1]
    count = na.shape[0]
    for i, tokens in enumerate((na, nb)):
        at = pl.ds(i * count, count)
        full = dot(tokens[...], w[...])
        a, b, c = full[:, :half], full[:, half : 2 * half], full[:, 2 * half :]
        outer[at, :] = a
        left[at, :] = b
        right[at, :] = c
        vals[at, :] = (b * c * mask[at, :]).astype(BF)
    owned = v0.shape[0]
    for k, out in enumerate((v0, v1, v2, v3)):
        out[...] = vals[rows_at((z + k) & 3, owned), :]


def neighbours(x, short, length):
    place = lax.broadcasted_iota(jnp.int32, x.shape, 0)
    starts = (place == 0) | (short & (place % SHORT_LENGTH == 0))
    ends = (place == length - 1) | (short & (place % SHORT_LENGTH == SHORT_LENGTH - 1))
    earlier = jnp.where(starts, 0.0, pltpu.roll(x, 1, 0))
    later = jnp.where(ends, 0.0, pltpu.roll(x, length - 1, 0))
    return earlier, later


def fold_kernel(where, v0, r1, r2, r3, table, flipped, base, gain, taps, vals, spectrum, cond_spec, o0, o1, o2, o3, triple, filtered, conv):
    z, short = where[0], where[3] == 1
    owned, half = v0.shape
    length = vals.shape[0]
    for k, piece in enumerate((v0, r1, r2, r3)):
        vals[rows_at((z - k) & 3, owned), :] = piece[...]
    wide = vals[...].astype(F32)
    before, after = neighbours(wide, short, length)
    cond = taps[0:1, :] * before + taps[1:2, :] * wide + taps[2:3, :] * after
    high = cond.astype(BF)
    triple[:, :half] = vals[...]
    triple[:, half : 2 * half] = high
    triple[:, 2 * half :] = (cond - high.astype(F32)).astype(BF)
    step = length // 2
    for i in range(2):
        at = pl.ds(i * step, step)
        folded = dot(table[at, :], triple[...])
        spec = folded[:, :half]
        cspec = folded[:, half : 2 * half] + folded[:, 2 * half :]
        spectrum[at, :] = spec
        cond_spec[at, :] = cspec
        kern = base[at, :] + gain[...] * (jnp.sqrt(cspec * cspec + 1.0) - 1.0)
        filtered[at, :] = (kern * spec).astype(BF)
    conv[...] = dot(flipped[...], filtered[...]).astype(BF)
    for k, out in enumerate((o0, o1, o2, o3)):
        out[...] = conv[rows_at((z + k) & 3, owned), :]


def mix_kernel(where, outer, c0, r1, r2, r3, w_rows, conv, mixed, own, other):
    z = where[0]
    owned = c0.shape[0]
    for k, piece in enumerate((c0, r1, r2, r3)):
        conv[rows_at((z - k) & 3, owned), :] = piece[...]
    mixed[...] = (outer[...] * conv[...].astype(F32)).astype(BF)
    count = own.shape[0]
    own[...] = dot(mixed[pl.ds(0, count), :], w_rows[...])
    other[...] = dot(mixed[pl.ds(count, count), :], w_rows[...]).astype(BF)


def second_kernel(where, x, own, came, gain, residual, normed):
    total = x[...] + own[...] + came[...].astype(F32)
    residual[...] = total
    hat, _ = norm_parts(total)
    normed[...] = (hat * gain[...]).astype(BF)


def feed_kernel(where, sa, sb, ca, cb, w_gu, w_dn, act, grads, own, other):
    half = act.shape[1]
    count = sa.shape[0]
    for i, (second, cot, out) in enumerate(((sa, ca, own), (sb, cb, other))):
        at = pl.ds(i * count, count)
        gate_up = dot(second[...], w_gu[...])
        gate, upward = gate_up[:, :half], gate_up[:, half:]
        grad_act = dot_nt(cot[...], w_dn[...])
        square = gate * gate
        tanh = jnp.tanh(GELU_A * gate * (1.0 + GELU_B * square))
        cdf = 0.5 * (1.0 + tanh)
        unit = gate * cdf
        slope = cdf + 0.5 * gate * (1.0 - tanh * tanh) * (GELU_A * (1.0 + 3.0 * GELU_B * square))
        act[at, :] = (unit * upward).astype(BF)
        grads[at, :half] = (grad_act * upward * slope).astype(BF)
        grads[at, half:] = (grad_act * unit).astype(BF)
        out[...] = dot_nt(grads[at, :], w_gu[...]).astype(out.dtype)


def down_kernel(where, a0, a1, a2, a3, w_dn, p0, p1, p2, p3, others):
    count = p0.shape[0]
    for m, (act, out) in enumerate(((a0, p0), (a1, p1), (a2, p2), (a3, p3))):
        out[...] = dot(act[pl.ds(0, count), :], w_dn[...]).astype(out.dtype)
        others[m] = dot(act[pl.ds(count, count), :], w_dn[...]).astype(BF)


def feed_weight_kernel(where, a0, a1, a2, a3, g0, g1, g2, g3, sa0, sa1, sa2, sa3, sb0, sb1, sb2, sb3, ca, cb, out, acts, grads, seconds, cots):
    chip = where[1]
    count, width = sa0.shape
    for m, (a, g, sa, sb) in enumerate(
        ((a0, g0, sa0, sb0), (a1, g1, sa1, sb1), (a2, g2, sa2, sb2), (a3, g3, sa3, sb3))
    ):
        at = pl.ds(m * 2 * count, 2 * count)
        acts[at, :] = a[...]
        grads[at, :] = g[...]
        seconds[pl.ds(m * 2 * count, count), :] = sa[...]
        seconds[pl.ds(m * 2 * count + count, count), :] = sb[...]
        cots[pl.ds(m * 2 * count, count), :] = ca[m]
        cots[pl.ds(m * 2 * count + count, count), :] = cb[m]
    nz, piece, _ = out.shape
    chunk = acts.shape[1] // 3
    rows = piece - chunk
    total = dot_tn(seconds[...], grads[...])
    for i in range(nz):
        out[i, pl.ds(0, rows), :] = total[i * rows : (i + 1) * rows].astype(BF)
    down = dot_tn(acts[...], cots[...])
    out[chip, pl.ds(rows, chunk), :] = jnp.zeros((chunk, width), BF)
    for i in range(3):
        to = i + (i >= chip).astype(jnp.int32)
        out[to, pl.ds(rows, chunk), :] = down[i * chunk : (i + 1) * chunk].astype(BF)


def second_back_kernel(where, residual, gain, cot, own, r1, r2, r3, grad_residual, low, grad_gain):
    grad = own[...] + r1[...].astype(F32) + r2[...].astype(F32) + r3[...].astype(F32)
    hat, inv = norm_parts(residual[...])
    pulled, grad_gain[...] = norm_pull(hat, inv, gain[...], grad)
    total = cot[...] + pulled
    grad_residual[...] = total
    low[...] = total.astype(BF)


def mix_back_kernel(where, ga, gb, w_rows, outer, conv, grad_outer, o0, o1, o2, o3, grad_conv):
    z = where[0]
    count = ga.shape[0]
    for i, grad in enumerate((ga, gb)):
        at = pl.ds(i * count, count)
        mixed = dot_nt(grad[...], w_rows[...])
        grad_outer[at, :] = (mixed * conv[at, :].astype(F32)).astype(BF)
        grad_conv[at, :] = (mixed * outer[at, :]).astype(BF)
    owned = o0.shape[0]
    for k, out in enumerate((o0, o1, o2, o3)):
        out[...] = grad_conv[rows_at((z + k) & 3, owned), :]


def fold_back_kernel(where, g0, r1, r2, r3, table, flipped, spectrum, cond_spec, base, gain, taps, vals, o0, o1, o2, o3, f0, f1, f2, f3, grads, double, filters):
    z, short = where[0], where[3] == 1
    owned, half = g0.shape
    length = vals.shape[0]
    for k, piece in enumerate((g0, r1, r2, r3)):
        grads[rows_at((z - k) & 3, owned), :] = piece[...]
    gf = dot(table[...], grads[...])
    cspec = cond_spec[...]
    root = jnp.sqrt(cspec * cspec + 1.0)
    above = root - 1.0
    grad_base = gf * spectrum[...]
    double[:, :half] = (gf * (base[...] + gain[...] * above)).astype(BF)
    double[:, half:] = (grad_base * gain[...] * (cspec / root)).astype(BF)
    unfolded = dot(flipped[...], double[...])
    grad_cond = unfolded[:, half:]
    wide = vals[...].astype(F32)
    before, after = neighbours(wide, short, length)
    grad_before, grad_after = neighbours(grad_cond, short, length)
    grads[...] = (
        unfolded[:, :half]
        + taps[0:1, :] * grad_after
        + taps[1:2, :] * grad_cond
        + taps[2:3, :] * grad_before
    ).astype(BF)
    for k, out in enumerate((o0, o1, o2, o3)):
        out[...] = grads[rows_at((z + k) & 3, owned), :]
    is_short = jnp.where(short, 1.0, 0.0)
    filters[pl.ds(0, length), :] = (grad_base * (1.0 - is_short)).astype(BF)
    folded = grad_base[:SHORT_LENGTH]
    for i in range(1, length // SHORT_LENGTH):
        folded = folded + grad_base[i * SHORT_LENGTH : (i + 1) * SHORT_LENGTH]
    filters[pl.ds(length, SHORT_LENGTH), :] = (folded * is_short).astype(BF)
    rest = filters.shape[0] - length - SHORT_LENGTH
    small = [
        jnp.sum(grad_base * above, axis=0, keepdims=True),
        jnp.sum(grad_cond * before, axis=0, keepdims=True),
        jnp.sum(grad_cond * wide, axis=0, keepdims=True),
        jnp.sum(grad_cond * after, axis=0, keepdims=True),
        jnp.zeros((rest - 4, half), F32),
    ]
    filters[pl.ds(length + SHORT_LENGTH, rest), :] = jnp.concatenate(small, axis=0).astype(BF)
    size = f0.shape[0]
    for k, out in enumerate((f0, f1, f2, f3)):
        out[...] = filters[rows_at((z + k) & 3, size), :]


def write_pieces(whole, outs, chip):
    rows = whole.shape[0] // 4
    quarter = rows // 4
    for m, out in enumerate(outs):
        for i in range(4):
            out[pl.ds(i * quarter, quarter), :] = whole[rows_at(i * 4 + (chip ^ m), quarter), :]


def late_kernel(where, g0, r1, r2, r3, left, right, mask, na, nb, late, p0, p1, p2, p3, grads, whole):
    z, chip = where[0], where[1]
    owned, half = g0.shape
    for k, piece in enumerate((g0, r1, r2, r3)):
        grads[rows_at((z - k) & 3, owned), :] = piece[...].astype(F32)
    count = na.shape[0]
    for i in range(2):
        at = pl.ds(i * count, count)
        grad = grads[at, :] * mask[at, :]
        late[at, :half] = (grad * right[at, :]).astype(BF)
        late[at, half:] = (grad * left[at, :]).astype(BF)
    total = dot_tn(na[...], late[pl.ds(0, count), :]) + dot_tn(nb[...], late[pl.ds(count, count), :])
    whole[...] = total.astype(BF)
    write_pieces(whole, (p0, p1, p2, p3), chip)


def early_kernel(where, na, nb, grad_outer, mixed, other_mixed, ga, gb, p0, p1, p2, p3, whole):
    chip, core = where[1], where[2]
    count = na.shape[0]
    half = mixed.shape[1]
    total = dot_tn(na[...], grad_outer[pl.ds(0, count), :])
    total = total + dot_tn(nb[...], grad_outer[pl.ds(count, count), :])
    whole[:, :half] = total.astype(BF)
    first = jnp.where(core == 0, ga[:, :half], ga[:, half:])
    second = jnp.where(core == 0, gb[:, :half], gb[:, half:])
    mine = dot_tn(mixed[pl.ds(0, count), :], first) + dot_tn(mixed[pl.ds(count, count), :], second)
    theirs = dot_tn(other_mixed[pl.ds(count, count), :], first)
    theirs = theirs + dot_tn(other_mixed[pl.ds(0, count), :], second)
    whole[rows_at(core, half), half:] = mine.astype(BF)
    whole[rows_at(1 - core, half), half:] = theirs.astype(BF)
    write_pieces(whole, (p0, p1, p2, p3), chip)


def first_grad_kernel(where, grad_outer, late, w, own, other):
    half = grad_outer.shape[1]
    count = own.shape[0]
    for i, out in enumerate((own, other)):
        at = pl.ds(i * count, count)
        total = dot_nt(grad_outer[at, :], w[:, :half]) + dot_nt(late[at, :], w[:, half:])
        out[...] = total.astype(out.dtype)


def first_back_kernel(where, x, gain, grad_residual, own, came, grad_inputs, grad_gain):
    grad = own[...] + came[...].astype(F32)
    hat, inv = norm_parts(x[...])
    pulled, grad_gain[...] = norm_pull(hat, inv, gain[...], grad)
    grad_inputs[...] = grad_residual[...] + pulled


def share_kernel(where, own, r1, r2, r3, ride, o0, o1, o2, o3, total):
    z = where[0]
    total[...] = (
        own[...].astype(F32) + r1[...].astype(F32) + r2[...].astype(F32) + r3[...].astype(F32)
    ).astype(BF)
    quarter = own.shape[0] // 4
    width = own.shape[1]
    first = lax.broadcasted_iota(jnp.int32, (RIDE, width), 0) == 0
    extra = jnp.where(first, jnp.broadcast_to(ride[...], (RIDE, width)), 0.0).astype(BF)
    for k, out in enumerate((o0, o1, o2, o3)):
        out[pl.ds(0, quarter), :] = total[rows_at((z + k) & 3, quarter), :]
        out[pl.ds(quarter, RIDE), :] = extra


def sum_kernel(where, own, r1, r2, r3, out):
    total = own[...].astype(F32) + r1[...].astype(F32) + r2[...].astype(F32) + r3[...].astype(F32)
    out[...] = total.astype(out.dtype)


def order_kernel(where, own, r1, r2, r3, out):
    chip = where[1]
    quarter = own.shape[0] - RIDE
    riding = jnp.zeros((1, own.shape[1]), F32)
    for m, piece in enumerate((own, r1, r2, r3)):
        out[rows_at(chip ^ m, quarter), :] = piece[pl.ds(0, quarter), :]
        riding = riding + piece[pl.ds(quarter, RIDE), :].astype(F32)[0:1]
    first = lax.broadcasted_iota(jnp.int32, (RIDE, own.shape[1]), 0) == 0
    extra = jnp.where(first, jnp.broadcast_to(riding, (RIDE, own.shape[1])), 0.0)
    out[pl.ds(4 * quarter, RIDE), :] = extra.astype(BF)


def feed_order_kernel(where, shares, gate_up, down):
    z = where[0]
    rows = gate_up.shape[0]
    chunk = shares.shape[1] - rows
    per_z = 6 * chunk
    for side in range(2):
        for zz in range(4):
            for c in range(6):
                mm = c if c < 2 * zz else c + 2
                at = (side * 3 + zz - (zz > mm // 2)) * chunk
                to = side * 4 * per_z + zz * per_z + c * chunk
                gate_up[:, to : to + chunk] = shares[mm, :rows, at : at + chunk].astype(F32)
    for c in range(6):
        mm = c + 2 * (c >= 2 * z).astype(jnp.int32)
        down[pl.ds(c * chunk, chunk), :] = shares[mm, pl.ds(rows, chunk), :].astype(F32)


def last_kernel(where, early, early_other, late, late_other, w_in, w_out):
    core = where[2]
    rows = w_in.shape[0]
    width = w_out.shape[1]
    half = width // 2
    for own, other, at, to, out in (
        (early, early_other, 0, 0, w_in),
        (late, late_other, 0, width, w_in),
        (late, late_other, half, 2 * width, w_in),
        (early, early_other, half, 0, w_out),
    ):
        a = own[:rows, at : at + half].astype(F32)
        b = other[:rows, at : at + half].astype(F32)
        out[:, to : to + half] = jnp.where(core == 0, a, b)
        out[:, to + half : to + width] = jnp.where(core == 0, b, a)


def body(
    inputs,
    cotangent,
    group,
    lens,
    norm1_gain,
    w_in,
    kernel_long,
    kernel_short,
    conv_weight,
    cond_gain,
    w_out,
    norm2_gain,
    w_gate_up,
    w_down,
):
    nz = lax.axis_size("freq")
    ndp = lax.axis_size("dp")
    z = lax.axis_index("freq")
    d = lax.axis_index("dp")
    core = d % 2
    chip = (d // 2) % 4
    member = d % GROUP
    owned, slots, width = inputs.shape
    half = width // 2
    length = owned * nz
    tokens = owned * slots
    rows = w_in.shape[0]
    quarter = rows // 4
    others = ndp // GROUP
    across = [[i + GROUP * g for g in range(others)] for i in range(GROUP)]
    blocks = [[g * GROUP + i for i in range(GROUP)] for g in range(others)]

    def core_swap(x):
        return lax.ppermute(x, "dp", [(i, i ^ 1) for i in range(ndp)])

    def chip_swap(x, m):
        return lax.ppermute(x, "dp", [(i, i ^ (2 * m)) for i in range(ndp)])

    def z_rot(x, k):
        return lax.ppermute(x, "freq", [(i, (i + k) % nz) for i in range(nz)])

    def mine(x, axis=-1):
        low, high = jnp.split(x, 2, axis=axis)
        return jnp.where(core == 0, low, high)

    def theirs(x, axis=-1):
        low, high = jnp.split(x, 2, axis=axis)
        return jnp.where(core == 0, high, low)

    def joined(own, other, axis=-1):
        return jnp.where(
            core == 0,
            jnp.concatenate([own, other], axis=axis),
            jnp.concatenate([other, own], axis=axis),
        )

    def from_z(rel):
        stacked = jnp.stack(rel)
        return jnp.concatenate([pick(stacked, (z - i) % nz) for i in range(nz)], axis=0)

    def z_swap(pieces):
        return [pieces[0]] + [z_rot(pieces[k], k) for k in range(1, nz)]

    def over_groups(x):
        if others > 1:
            return lax.psum(x, "dp", axis_index_groups=across)
        return x

    def in_cols(x):
        return jnp.concatenate([mine(x[:, i * width : (i + 1) * width]) for i in range(3)], axis=1)

    near = in_cols(lax.dynamic_slice_in_dim(w_in, chip * quarter, quarter, axis=0))
    in_near = [z_rot(near, k) for k in range(1, nz)]
    in_stack = jnp.stack(in_near)
    in_far = [chip_swap(in_stack, m) for m in (1, 2, 3)]

    out_local = mine(w_out)
    out_piece = lax.dynamic_slice_in_dim(out_local, chip * quarter, quarter, axis=0)
    out_near = [z_rot(out_piece, k) for k in range(1, nz)]
    out_stack = jnp.stack(out_near)
    out_far = [chip_swap(out_stack, m) for m in (1, 2, 3)]
    rel = [out_local]
    for k in range(nz - 1):
        by_chip = jnp.stack([out_near[k]] + [piece[k] for piece in out_far])
        rel.append(jnp.concatenate([pick(by_chip, chip ^ i) for i in range(4)], axis=0))
    out_cols = from_z(rel)
    w_out_rows = joined(mine(out_cols, 0), core_swap(theirs(out_cols, 0)))

    filt_piece = jnp.concatenate([mine(kernel_long), mine(kernel_short)], axis=0)
    filt_rel = z_swap([filt_piece] * nz)
    long_base = from_z([x[:owned] for x in filt_rel])
    short_base = from_z([x[owned:] for x in filt_rel])

    hidden = w_down.shape[0] * nz
    per_z = w_down.shape[0]
    chunk = per_z // 6

    def chunk_of(zz):
        return jnp.where(member < 2 * zz, member, member - 2)

    pieces = []
    for side in range(2):
        for i in range(3):
            zz = i + (i >= chip).astype(jnp.int32)
            start = side * hidden + zz * per_z + chunk_of(zz) * chunk
            pieces.append(lax.dynamic_slice_in_dim(w_gate_up, start, chunk, axis=1))
    down_piece = lax.dynamic_slice_in_dim(
        w_down, jnp.clip(chunk_of(z), 0, 5) * chunk, chunk, axis=0
    )
    mlp_piece = jnp.concatenate([jnp.concatenate(pieces, axis=1), down_piece], axis=0)
    mlp_all = lax.all_gather(mlp_piece, "freq", axis=0)
    w_gu = mlp_all[:, :rows].reshape(width, width)
    down_four = mlp_all[:, rows:]
    w_dn = jnp.concatenate(
        [pick(down_four, i + (i >= chip).astype(jnp.int32)) for i in range(3)], axis=0
    )

    x_own = jnp.swapaxes(inputs, 0, 1).reshape(tokens, width)
    cot_own = jnp.swapaxes(cotangent, 0, 1).reshape(tokens, width)
    cot_low = cot_own.astype(BF)
    cot_near = jnp.stack([cot_low] + [chip_swap(cot_low, m) for m in (1, 2, 3)])
    cot_far = core_swap(cot_near)

    marks = jnp.concatenate([group[:, None], lens], axis=1)
    marks = jnp.concatenate([marks, core_swap(marks)], axis=0)
    group_all = marks[:, 0]
    lens_all = marks[:, 1:]
    posit = z * owned + jnp.arange(owned, dtype=jnp.int32)
    hit = (posit // SHORT_LENGTH)[None, :, None] == jnp.arange(lens.shape[1], dtype=jnp.int32)
    quarter_len = jnp.sum(jnp.where(hit, lens_all[:, None, :], 0), axis=2)
    mask = jnp.where(
        group_all[:, None] == 1,
        (posit % SHORT_LENGTH)[None, :] < quarter_len,
        posit[None, :] < jnp.sum(lens_all, axis=1)[:, None],
    )
    mask = mask.astype(F32).reshape(2 * tokens, 1)
    slot_group = pick(group_all, z)
    where = jnp.stack([z, chip, core, slot_group, z, z, z, z]).astype(jnp.int32)

    repeat = length // SHORT_LENGTH
    long_table = cosine_table(length)
    short_table = np.kron(np.eye(repeat), cosine_table(SHORT_LENGTH)).astype(np.float32)
    is_short = slot_group == 1
    table = jnp.where(is_short, jnp.asarray(short_table, BF), jnp.asarray(long_table, BF))
    flipped = jnp.where(is_short, jnp.asarray(short_table.T, BF), jnp.asarray(long_table.T, BF))
    base = jnp.where(is_short, jnp.tile(short_base, (repeat, 1)), long_base).astype(F32)
    gain_half = mine(cond_gain)[None]
    taps = mine(conv_weight)
    gain_one = norm1_gain[None]
    gain_two = norm2_gain[None]

    hat_one, _ = norm_parts(x_own)
    normed = (hat_one * gain_one).astype(BF)
    normed_other = core_swap(normed)
    piece = ((owned, half), BF)
    many = 2 * tokens
    w_in_half, outer, left, right, *sends = run(
        project_kernel,
        "project",
        [((width, 3 * half), BF)] + [((many, half), F32)] * 3 + [piece] * 4,
        where,
        [normed, normed_other, in_cols(w_in), *in_near, *in_far, mask],
        [pltpu.VMEM((many, half), BF)],
        flops=2 * many * width * 3 * half,
    )
    came = z_swap(sends)
    vals, spectrum, cond_spec, *sends = run(
        fold_kernel,
        "fold",
        [((length, half), BF)] + [((length, half), F32)] * 2 + [piece] * 4,
        where,
        [*came, table, flipped, base, gain_half, taps],
        [
            pltpu.VMEM((length, 3 * half), BF),
            pltpu.VMEM((length, half), BF),
            pltpu.VMEM((length, half), BF),
        ],
        flops=2 * length * length * 4 * half,
    )
    came = z_swap(sends)
    conv, mixed, part_own, part_other = run(
        mix_kernel,
        "mix",
        [((many, half), BF)] * 2 + [((tokens, width), F32), ((tokens, width), BF)],
        where,
        [outer, *came, w_out_rows],
        flops=2 * many * half * width,
    )
    residual, normed_two = run(
        second_kernel,
        "second_norm",
        [((tokens, width), F32), ((tokens, width), BF)],
        where,
        [x_own, part_own, core_swap(part_other), gain_two],
        flops=tokens * width * 12,
    )

    arrived = [normed_two] + [chip_swap(normed_two, m) for m in (1, 2, 3)]
    seconds, acts, grads_gu, sums = [], [], [], []
    order = ()
    for m in range(4):
        second = core_swap(arrived[m])
        act, grad_gu, own, other = run(
            feed_kernel,
            "feed",
            [((many, half), BF), ((many, width), BF), ((tokens, width), F32), ((tokens, width), BF)],
            where,
            [arrived[m], second, cot_near[m], cot_far[m], w_gu, w_dn],
            after=order,
            flops=2 * many * width * (2 * width + half),
        )
        order = (act,)
        seconds.append(second)
        acts.append(act)
        grads_gu.append(grad_gu)
        sums.append(own + core_swap(other).astype(F32))
    backs = [chip_swap(sums[m].astype(BF), m) for m in (1, 2, 3)]
    grad_residual, grad_mix, grad_gain_two = run(
        second_back_kernel,
        "second_norm_back",
        [((tokens, width), F32), ((tokens, width), BF), ((1, width), F32)],
        where,
        [residual, gain_two, cot_own, sums[0], *backs],
        flops=tokens * width * 30,
    )
    grad_mix_other = core_swap(grad_mix)
    grad_outer, *sends = run(
        mix_back_kernel,
        "mix_back",
        [((many, half), BF)] + [piece] * 4,
        where,
        [grad_mix, grad_mix_other, w_out_rows, outer, conv],
        [pltpu.VMEM((many, half), BF)],
        flops=2 * many * half * width,
    )
    came = z_swap(sends)

    mlp_grads = run(
        feed_weight_kernel,
        "feed_weights",
        [((nz, rows + chunk, width), BF)],
        where,
        [*acts, *grads_gu, *arrived, *seconds, cot_near, cot_far],
        [
            pltpu.VMEM((4 * many, half), BF),
            pltpu.VMEM((4 * many, width), BF),
            pltpu.VMEM((4 * many, width), BF),
            pltpu.VMEM((4 * many, width), BF),
        ],
        after=(grad_outer,),
        flops=2 * 4 * many * width * (width + half),
    )[0]
    mlp_share = lax.psum_scatter(mlp_grads, "freq", scatter_dimension=0, tiled=False)
    mlp_share = over_groups(mlp_share)
    mlp_sum = lax.all_gather(mlp_share, "dp", axis=0, axis_index_groups=blocks)
    grad_w_gate_up, grad_w_down = run(
        feed_order_kernel,
        "feed_order",
        [((rows, 2 * hidden), F32), ((per_z, width), F32)],
        where,
        [mlp_sum],
    )

    def shares(parts, ride):
        total = [parts[0]] + [chip_swap(parts[m], m) for m in (1, 2, 3)]
        sends = run(
            share_kernel,
            "share",
            [((quarter + RIDE, width), BF)] * 4,
            where,
            [*total, ride],
            [pltpu.VMEM((rows, width), BF)],
        )
        piece = run(sum_kernel, "sum", [((quarter + RIDE, width), BF)], where, z_swap(sends))[0]
        piece = over_groups(piece)
        rel = [piece] + [chip_swap(piece, m) for m in (1, 2, 3)]
        own = run(order_kernel, "order", [((rows + RIDE, width), BF)], where, rel)[0]
        return own, core_swap(own)

    parts = run(
        early_kernel,
        "early_weights",
        [((rows, width), BF)] * 4,
        where,
        [normed, normed_other, grad_outer, mixed, core_swap(mixed), grad_mix, grad_mix_other],
        [pltpu.VMEM((width, width), BF)],
        after=(mlp_grads,),
        flops=2 * many * width * width,
    )
    early, early_other = shares(parts, grad_gain_two)

    fill = -(length + SHORT_LENGTH + 4) % (nz * 16)
    size = (length + SHORT_LENGTH + 4 + fill) // nz
    *sends, f0, f1, f2, f3 = run(
        fold_back_kernel,
        "fold_back",
        [piece] * 4 + [((size, half), BF)] * 4,
        where,
        [*came, table, flipped, spectrum, cond_spec, base, gain_half, taps, vals],
        [
            pltpu.VMEM((length, half), BF),
            pltpu.VMEM((length, 2 * half), BF),
            pltpu.VMEM((size * nz, half), BF),
        ],
        flops=2 * length * length * 3 * half,
    )
    came = z_swap(sends)
    late, *parts = run(
        late_kernel,
        "late_weights",
        [((many, width), BF)] + [((rows, width), BF)] * 4,
        where,
        [*came, left, right, mask, normed, normed_other],
        [pltpu.VMEM((many, half), F32), pltpu.VMEM((width, width), BF)],
        flops=2 * many * width * width,
    )
    own, other = run(
        first_grad_kernel,
        "first_grad",
        [((tokens, width), F32), ((tokens, width), BF)],
        where,
        [grad_outer, late, w_in_half],
        flops=2 * many * width * 3 * half,
    )
    grad_inputs, grad_gain_one = run(
        first_back_kernel,
        "first_norm_back",
        [((tokens, width), F32), ((1, width), F32)],
        where,
        [x_own, gain_one, grad_residual, own, core_swap(other)],
        flops=tokens * width * 30,
    )
    late_own, late_other = shares(parts, grad_gain_one)

    low = run(sum_kernel, "sum", [((size, half), BF)], where, z_swap([f0, f1, f2, f3]))[0]
    near = [low] + [chip_swap(low, m) for m in (1, 2, 3)]
    low = run(sum_kernel, "sum", [((size, half), BF)], where, near)[0]
    low = over_groups(low)
    filt_own = from_z(z_swap([low] * nz))
    filt = joined(filt_own, core_swap(filt_own)).astype(F32)
    tail = filt[length + SHORT_LENGTH :]

    p0, p1, p2, p3, far = run(
        down_kernel,
        "down",
        [((tokens, width), F32)] * 4 + [((4, tokens, width), BF)],
        where,
        [*acts, w_dn],
        after=(parts[0],),
        flops=2 * 4 * many * width * half,
    )
    far = core_swap(far)
    layer_out = residual + p0 + far[0].astype(F32)
    for m, part in ((1, p1), (2, p2), (3, p3)):
        part = (part + far[m].astype(F32)).astype(BF)
        layer_out = layer_out + chip_swap(part, m).astype(F32)

    grad_w_in, grad_w_out = run(
        last_kernel,
        "last",
        [((rows, 3 * width), F32), ((rows, width), F32)],
        where,
        [early, early_other, late_own, late_other],
    )

    def riding(own, other):
        return own[rows].astype(F32) + other[rows].astype(F32)

    def placed(x):
        return jnp.swapaxes(x.reshape(slots, owned, width), 0, 1)

    return (
        placed(layer_out),
        placed(grad_inputs),
        riding(late_own, late_other),
        grad_w_in,
        filt[:length],
        filt[length : length + SHORT_LENGTH],
        tail[1:4],
        tail[0],
        grad_w_out,
        riding(early, early_other),
        grad_w_gate_up,
        grad_w_down,
    )


def solution(mesh):
    return jax.shard_map(
        body,
        mesh=mesh,
        in_specs=(
            P("freq", "dp", None),
            P("freq", "dp", None),
            P("dp"),
            P("dp", None),
            P(),
            P("freq", None),
            P("freq", None),
            P("freq", None),
            P(),
            P(),
            P("freq", None),
            P(),
            P("freq", None),
            P("freq", None),
        ),
        out_specs=(
            P("freq", "dp", None),
            P("freq", "dp", None),
            P(),
            P("freq", None),
            P(),
            P(),
            P(),
            P(),
            P("freq", None),
            P(),
            P("freq", None),
            P("freq", None),
        ),
        check_vma=False,
    )
```

profile of v0, /device:TPU:0, one launch (start us, length us, event | category | flops | bytes accessed | tf_op | source)
XLA Modules:
  0.0 420.7 jit_solution(4999384582092801883)
XLA Ops:
  8.9 5.0 %collective-permute-start.4 = (bf16[48,1152]{1,0:T(8,128)(2,1)}, bf16[48,1152]{1,0:T(8,128)(2,1)S(1)}, u32[]{:S(2)}, u32[]{:S(2)}) collective-permute-start(bf16[48,1152]{1,0:T(8,128)(2,1)} %pad_maximum_fusion.15), channel_id=1, source_target_pairs={{0,3},{1,0},{2,1},{3,2},{4,7},{5,4},{6,5},{7,6},{8,11},{9,8},{10,9... | collective-permute-start | bytes 331784 | tf_op jit(solution)/shard_map/ppermute | solution.py:447
  44.6 3.8 collective-permute-start.13
  59.4 14.3 %collective-permute-done.12 = bf16[160,384]{1,0:T(8,128)(2,1)S(1)} collective-permute-done((bf16[160,384]{1,0:T(8,128)(2,1)}, bf16[160,384]{1,0:T(8,128)(2,1)S(1)}, u32[]{:S(2)}, u32[]{:S(2)}) %collective-permute-start.12) | collective-permute-done | bytes 122912 | tf_op jit(solution)/shard_map/ppermute | solution.py:447
  76.7 3.6 collective-permute-done.22
  100.4 4.4 %collective-permute-done.6.refs_8_ = bf16[3,48,1152]{2,1,0:T(8,128)(2,1)S(1)} collective-permute-done((bf16[3,48,1152]{2,1,0:T(8,128)(2,1)S(1)}, bf16[3,48,1152]{2,1,0:T(8,128)(2,1)S(1)}, u32[]{:S(2)}, u32[]{:S(2)}) %collective-permute-start.6) | collective-permute-done | bytes 331808 | tf_op jit(solution)/shard_map/ppermute | solution.py:444
  104.9 3.5 project.1
  142.2 9.7 %collective-permute-done.34.refs_1_.refs_12_ = bf16[256,768]{1,0:T(8,128)(2,1)} collective-permute-done((bf16[256,768]{1,0:T(8,128)(2,1)}, bf16[256,768]{1,0:T(8,128)(2,1)}, u32[]{:S(2)}, u32[]{:S(2)}) %collective-permute-start.34) | collective-permute-done | bytes 393248 | tf_op jit(solution)/shard_map/ppermute | solution.py:444
  151.9 7.6 %collective-permute-done.32.refs_1_.refs_11_ = bf16[256,768]{1,0:T(8,128)(2,1)} collective-permute-done((bf16[256,768]{1,0:T(8,128)(2,1)}, bf16[256,768]{1,0:T(8,128)(2,1)}, u32[]{:S(2)}, u32[]{:S(2)}) %collective-permute-start.32) | collective-permute-done | bytes 393248 | tf_op jit(solution)/shard_map/ppermute | solution.py:444
  167.4 4.5 %feed.4 = (bf16[512,384]{1,0:T(8,128)(2,1)S(1)}, bf16[512,768]{1,0:T(8,128)(2,1)S(1)}, f32[256,768]{1,0:T(8,128)}, bf16[256,768]{1,0:T(8,128)(2,1)S(1)}) custom-call(s32[8]{0:T(128)S(1)} %stack.129.refs_0_, bf16[256,768]{1,0:T(8,128)(2,1)} %get-tuple-element.107.refs_1_.refs_9_, bf16[256,768]{1,0:T(8,128)(2,1)} %collective-permute-done.25.refs_2_.refs_13_, ...), custom_call_target="tpu_custom_call" | custom-call | flops 1509949440 | bytes 5701632 | tf_op jit(solution)/shard_map/feed/pallas_call | solution.py:67
  172.8 4.5 %feed.5 = (bf16[512,384]{1,0:T(8,128)(2,1)S(1)}, bf16[512,768]{1,0:T(8,128)(2,1)}, f32[256,768]{1,0:T(8,128)}, bf16[256,768]{1,0:T(8,128)(2,1)S(1)}) custom-call(s32[8]{0:T(128)S(1)} %stack.129.refs_0_, bf16[256,768]{1,0:T(8,128)(2,1)} %collective-permute-done.30.refs_1_.refs_10_, bf16[256,768]{1,0:T(8,128)(2,1)} %collective-permute-done.31.refs_2_.refs_14_, ...), custom_call_target="tpu_custom_call" | custom-call | flops 1509949440 | bytes 5701632 | tf_op jit(solution)/shard_map/feed/pallas_call | solution.py:67
  177.3 4.4 %feed.6 = (bf16[512,384]{1,0:T(8,128)(2,1)S(1)}, bf16[512,768]{1,0:T(8,128)(2,1)}, f32[256,768]{1,0:T(8,128)}, bf16[256,768]{1,0:T(8,128)(2,1)S(1)}) custom-call(s32[8]{0:T(128)S(1)} %stack.129.refs_0_, bf16[256,768]{1,0:T(8,128)(2,1)} %collective-permute-done.32.refs_1_.refs_11_, bf16[256,768]{1,0:T(8,128)(2,1)} %collective-permute-done.33.refs_2_.refs_15_, ...), custom_call_target="tpu_custom_call" | custom-call | flops 1509949440 | bytes 5701632 | tf_op jit(solution)/shard_map/feed/pallas_call | solution.py:67
  181.8 4.4 %feed.7 = (bf16[512,384]{1,0:T(8,128)(2,1)S(1)}, bf16[512,768]{1,0:T(8,128)(2,1)}, f32[256,768]{1,0:T(8,128)}, bf16[256,768]{1,0:T(8,128)(2,1)S(1)}) custom-call(s32[8]{0:T(128)S(1)} %stack.129.refs_0_, bf16[256,768]{1,0:T(8,128)(2,1)} %collective-permute-done.34.refs_1_.refs_12_, bf16[256,768]{1,0:T(8,128)(2,1)} %collective-permute-done.35.refs_2_.refs_16_, ...), custom_call_target="tpu_custom_call" | custom-call | flops 1509949440 | bytes 5701632 | tf_op jit(solution)/shard_map/feed/pallas_call | solution.py:67
  192.1 7.2 %collective-permute-done.38.refs_5_ = bf16[256,768]{1,0:T(8,128)(2,1)S(1)} collective-permute-done((bf16[256,768]{1,0:T(8,128)(2,1)S(1)}, bf16[256,768]{1,0:T(8,128)(2,1)S(1)}, u32[]{:S(2)}, u32[]{:S(2)}) %collective-permute-start.38) | collective-permute-done | bytes 393248 | tf_op jit(solution)/shard_map/ppermute | solution.py:444
  199.2 7.8 %collective-permute-done.42.refs_7_ = bf16[256,768]{1,0:T(8,128)(2,1)S(1)} collective-permute-done((bf16[256,768]{1,0:T(8,128)(2,1)S(1)}, bf16[256,768]{1,0:T(8,128)(2,1)S(1)}, u32[]{:S(2)}, u32[]{:S(2)}) %collective-permute-start.42) | collective-permute-done | bytes 393248 | tf_op jit(solution)/shard_map/ppermute | solution.py:444
  218.0 9.2 %feed_weights.1.refs_8_ = bf16[4,320,768]{2,1,0:T(8,128)(2,1)} custom-call(s32[8]{0:T(128)S(1)} %stack.129.refs_0_, bf16[512,384]{1,0:T(8,128)(2,1)S(1)} %get-tuple-element.108.refs_7_.refs_1_, bf16[512,384]{1,0:T(8,128)(2,1)S(1)} %get-tuple-element.109.refs_7_.refs_2_, bf16[512,384]{1,0:T(8,128)(2,1)S(1)} %get-tuple-element.110.refs_7_.refs_3_, ...), custom_call_target="tpu_custom_call" | custom-call | flops 3623878656 | bytes 12976128 | tf_op jit(solution)/shard_map/feed_weights/pallas_call | solution.py:67
  227.4 40.2 %reduce-scatter.2.cloned.1.call-done = bf16[1,320,768]{2,1,0:T(8,128)(2,1)} async-done(((bf16[4,320,768]{2,1,0:T(8,128)(2,1)}), bf16[1,320,768]{2,1,0:T(8,128)(2,1)}) %reduce-scatter.2.cloned.1.call-update) | async-done | bytes 491536 | tf_op jit(solution)/shard_map/reduce_scatter | solution.py:660
  275.3 3.7 collective-permute-done.45.refs_3_
  280.0 3.4 fold_back.1
  296.4 3.8 down.1
  308.2 7.4 %collective-permute-done.68.refs_4_ = bf16[192,768]{1,0:T(8,128)(2,1)S(1)} collective-permute-done((bf16[192,768]{1,0:T(8,128)(2,1)S(1)}, bf16[192,768]{1,0:T(8,128)(2,1)S(1)}, u32[]{:S(2)}, u32[]{:S(2)}) %collective-permute-start.68) | collective-permute-done | bytes 294944 | tf_op jit(solution)/shard_map/ppermute | solution.py:444
  342.0 5.0 %collective-permute-done.83 = bf16[176,384]{1,0:T(8,128)(2,1)S(1)} collective-permute-done((bf16[176,384]{1,0:T(8,128)(2,1)S(1)}, bf16[176,384]{1,0:T(8,128)(2,1)S(1)}, u32[]{:S(2)}, u32[]{:S(2)}) %collective-permute-start.83) | collective-permute-done | bytes 135200 | tf_op jit(solution)/shard_map/ppermute | solution.py:447
  351.8 8.6 %collective-permute-done.56.refs_3_ = bf16[192,768]{1,0:T(8,128)(2,1)S(1)} collective-permute-done((bf16[192,768]{1,0:T(8,128)(2,1)S(1)}, bf16[192,768]{1,0:T(8,128)(2,1)S(1)}, u32[]{:S(2)}, u32[]{:S(2)}) %collective-permute-start.56) | collective-permute-done | bytes 294944 | tf_op jit(solution)/shard_map/ppermute | solution.py:444
  394.6 9.8 %collective-permute-done.53 = bf16[256,768]{1,0:T(8,128)(2,1)S(1)} collective-permute-done((bf16[256,768]{1,0:T(8,128)(2,1)S(1)}, bf16[256,768]{1,0:T(8,128)(2,1)S(1)}, u32[]{:S(2)}, u32[]{:S(2)}) %collective-permute-start.53) | collective-permute-done | bytes 393248 | tf_op jit(solution)/shard_map/ppermute | solution.py:444
  409.7 4.0 feed_order.1
  (470 shorter events, 225.2 us)
Async XLA Ops:
  7.2 155.3 %all-gather.6.cloned.1.call-start = ((), (), s32[]{:S(2)}) async-start(), calls=%async_computation.3 | async-start | bytes 2457600 | tf_op jit(solution)/shard_map/all_gather | solution.py:518
  8.9 40.3 %collective-permute-start.4 = (bf16[48,1152]{1,0:T(8,128)(2,1)}, bf16[48,1152]{1,0:T(8,128)(2,1)S(1)}, u32[]{:S(2)}, u32[]{:S(2)}) collective-permute-start(bf16[48,1152]{1,0:T(8,128)(2,1)} %pad_maximum_fusion.15), channel_id=1, source_target_pairs={{0,3},{1,0},{2,1},{3,2},{4,7},{5,4},{6,5},{7,6},{8,11},{9,8},{10,9... | collective-permute-start | bytes 331784 | tf_op jit(solution)/shard_map/ppermute | solution.py:447
  14.0 35.9 %collective-permute-start.3 = (bf16[48,1152]{1,0:T(8,128)(2,1)}, bf16[48,1152]{1,0:T(8,128)(2,1)S(1)}, u32[]{:S(2)}, u32[]{:S(2)}) collective-permute-start(bf16[48,1152]{1,0:T(8,128)(2,1)} %pad_maximum_fusion.15), channel_id=1, source_target_pairs={{0,2},{1,3},{2,0},{3,1},{4,6},{5,7},{6,4},{7,5},{8,10},{9,11},{10,... | collective-permute-start | bytes 331784 | tf_op jit(solution)/shard_map/ppermute | solution.py:447
  15.6 28.9 %collective-permute-start.19 = (bf16[48,384]{1,0:T(8,128)(2,1)}, bf16[48,384]{1,0:T(8,128)(2,1)S(1)}, u32[]{:S(2)}, u32[]{:S(2)}) collective-permute-start(bf16[48,384]{1,0:T(8,128)(2,1)} %constant_dynamic-slice_fusion.1), channel_id=1, source_target_pairs={{0,3},{1,0},{2,1},{3,2},{4,7},{5,4},{6,5},{7,6},{8,11},{9,8},{10,9... | collective-permute-start | bytes 110600 | tf_op jit(solution)/shard_map/ppermute | solution.py:447
  16.1 28.5 %collective-permute-start.18 = (bf16[48,384]{1,0:T(8,128)(2,1)}, bf16[48,384]{1,0:T(8,128)(2,1)}, u32[]{:S(2)}, u32[]{:S(2)}) collective-permute-start(bf16[48,384]{1,0:T(8,128)(2,1)} %constant_dynamic-slice_fusion.1), channel_id=1, source_target_pairs={{0,2},{1,3},{2,0},{3,1},{4,6},{5,7},{6,4},{7,5},{8,10},{9,11},{10,... | collective-permute-start | bytes 110600 | tf_op jit(solution)/shard_map/ppermute | solution.py:447
  26.4 241.2 %reduce-scatter.2.cloned.1.call-start = ((), (), s32[]{:S(2)}) async-start(), calls=%async_computation.1 | async-start | bytes 2457600 | tf_op jit(solution)/shard_map/reduce_scatter | solution.py:660
  48.4 25.4 %collective-permute-start.12 = (bf16[160,384]{1,0:T(8,128)(2,1)}, bf16[160,384]{1,0:T(8,128)(2,1)S(1)}, u32[]{:S(2)}, u32[]{:S(2)}) collective-permute-start(bf16[160,384]{1,0:T(8,128)(2,1)} %pad_maximum_fusion.14), channel_id=1, source_target_pairs={{0,2},{1,3},{2,0},{3,1},{4,6},{5,7},{6,4},{7,5},{8,10},{9,11},{10,... | collective-permute-start | bytes 368648 | tf_op jit(solution)/shard_map/ppermute | solution.py:447
  49.2 24.8 %collective-permute-start.11 = (bf16[160,384]{1,0:T(8,128)(2,1)}, bf16[160,384]{1,0:T(8,128)(2,1)S(1)}, u32[]{:S(2)}, u32[]{:S(2)}) collective-permute-start(bf16[160,384]{1,0:T(8,128)(2,1)} %pad_maximum_fusion.14), channel_id=1, source_target_pairs={{0,1},{1,2},{2,3},{3,0},{4,5},{5,6},{6,7},{7,4},{8,9},{9,10},{10,1... | collective-permute-start | bytes 368648 | tf_op jit(solution)/shard_map/ppermute | solution.py:447
  49.9 44.2 %collective-permute-start.28 = (bf16[256,768]{1,0:T(8,128)(2,1)S(1)}, bf16[256,768]{1,0:T(8,128)(2,1)S(1)}, u32[]{:S(2)}, u32[]{:S(2)}) collective-permute-start(bf16[256,768]{1,0:T(8,128)(2,1)S(1)} %bitcast_convert_fusion.refs_3_), channel_id=1, source_target_pairs={{0,24},{4,28},{8,16},{12,20},{16,8},{20,12},{24,0},{28,4},{1,25},{... | collective-permute-start | bytes 1179656 | tf_op jit(solution)/shard_map/ppermute | solution.py:444
  54.8 39.9 %collective-permute-start.27 = (bf16[256,768]{1,0:T(8,128)(2,1)S(1)}, bf16[256,768]{1,0:T(8,128)(2,1)S(1)}, u32[]{:S(2)}, u32[]{:S(2)}) collective-permute-start(bf16[256,768]{1,0:T(8,128)(2,1)S(1)} %bitcast_convert_fusion.refs_3_), channel_id=1, source_target_pairs={{0,16},{4,20},{8,24},{12,28},{16,0},{20,4},{24,8},{28,12},{1,17},{... | collective-permute-start | bytes 1179656 | tf_op jit(solution)/shard_map/ppermute | solution.py:444
  57.9 37.4 %collective-permute-start.26 = (bf16[256,768]{1,0:T(8,128)(2,1)S(1)}, bf16[256,768]{1,0:T(8,128)(2,1)S(1)}, u32[]{:S(2)}, u32[]{:S(2)}) collective-permute-start(bf16[256,768]{1,0:T(8,128)(2,1)S(1)} %bitcast_convert_fusion.refs_3_), channel_id=1, source_target_pairs={{0,8},{4,12},{8,0},{12,4},{16,24},{20,28},{24,16},{28,20},{1,9},{5... | collective-permute-start | bytes 1179656 | tf_op jit(solution)/shard_map/ppermute | solution.py:444
  73.8 24.6 %collective-permute-start.1 = (bf16[256,768]{1,0:T(8,128)(2,1)S(1)}, bf16[256,768]{1,0:T(8,128)(2,1)S(1)}, u32[]{:S(2)}, u32[]{:S(2)}) collective-permute-start(bf16[256,768]{1,0:T(8,128)(2,1)S(1)} %multiply_convert_fusion.refs_1_.refs_8_), channel_id=1, source_target_pairs={{0,4},{4,0},{8,12},{12,8},{16,20},{20,16},{24,28},{28,24},{1,5},{5... | collective-permute-start | bytes 1179656 | tf_op jit(solution)/shard_map/ppermute | solution.py:441
  98.2 61.8 %collective-permute-start.29 = (bf16[4,256,768]{2,1,0:T(8,128)(2,1)}, bf16[4,256,768]{2,1,0:T(8,128)(2,1)}, u32[]{:S(2)}, u32[]{:S(2)}) collective-permute-start(bf16[4,256,768]{2,1,0:T(8,128)(2,1)} %pad_maximum_fusion.refs_17_), channel_id=1, source_target_pairs={{0,4},{4,0},{8,12},{12,8},{16,20},{20,16},{24,28},{28,24},{1,5},{5... | collective-permute-start | bytes 4718600 | tf_op jit(solution)/shard_map/ppermute | solution.py:441
  98.4 29.2 %collective-permute-start.23 = (bf16[384,384]{1,0:T(8,128)(2,1)S(1)}, bf16[384,384]{1,0:T(8,128)(2,1)S(1)}, u32[]{:S(2)}, u32[]{:S(2)}) collective-permute-start(bf16[384,384]{1,0:T(8,128)(2,1)S(1)} %get-tuple-element.195), channel_id=1, source_target_pairs={{0,4},{4,0},{8,12},{12,8},{16,20},{20,16},{24,28},{28,24},{1,5},{5... | collective-permute-start | bytes 884744 | tf_op jit(solution)/shard_map/ppermute | solution.py:441
  140.8 18.7 %collective-permute-start.32 = (bf16[256,768]{1,0:T(8,128)(2,1)}, bf16[256,768]{1,0:T(8,128)(2,1)}, u32[]{:S(2)}, u32[]{:S(2)}) collective-permute-start(bf16[256,768]{1,0:T(8,128)(2,1)} %get-tuple-element.107.refs_1_.refs_9_), channel_id=1, source_target_pairs={{0,16},{4,20},{8,24},{12,28},{16,0},{20,4},{24,8},{28,12},{1,17},{... | collective-permute-start | bytes 1179656 | tf_op jit(solution)/shard_map/ppermute | solution.py:444
  142.1 24.0 %collective-permute-start.25 = (bf16[256,768]{1,0:T(8,128)(2,1)}, bf16[256,768]{1,0:T(8,128)(2,1)}, u32[]{:S(2)}, u32[]{:S(2)}) collective-permute-start(bf16[256,768]{1,0:T(8,128)(2,1)} %get-tuple-element.107.refs_1_.refs_9_), channel_id=1, source_target_pairs={{0,4},{4,0},{8,12},{12,8},{16,20},{20,16},{24,28},{28,24},{1,5},{5... | collective-permute-start | bytes 1179656 | tf_op jit(solution)/shard_map/ppermute | solution.py:441
  151.9 29.9 %collective-permute-start.35 = (bf16[256,768]{1,0:T(8,128)(2,1)}, bf16[256,768]{1,0:T(8,128)(2,1)}, u32[]{:S(2)}, u32[]{:S(2)}) collective-permute-start(bf16[256,768]{1,0:T(8,128)(2,1)} %collective-permute-done.34.refs_1_.refs_12_), channel_id=1, source_target_pairs={{0,4},{4,0},{8,12},{12,8},{16,20},{20,16},{24,28},{28,24},{1,5},{5... | collective-permute-start | bytes 1179656 | tf_op jit(solution)/shard_map/ppermute | solution.py:441
  190.0 19.6 %collective-permute-start.40 = (bf16[256,768]{1,0:T(8,128)(2,1)S(1)}, bf16[256,768]{1,0:T(8,128)(2,1)S(1)}, u32[]{:S(2)}, u32[]{:S(2)}) collective-permute-start(bf16[256,768]{1,0:T(8,128)(2,1)S(1)} %add_convert_fusion.1), channel_id=1, source_target_pairs={{0,16},{4,20},{8,24},{12,28},{16,0},{20,4},{24,8},{28,12},{1,17},{... | collective-permute-start | bytes 1179656 | tf_op jit(solution)/shard_map/ppermute | solution.py:444
  227.3 180.3 %all-gather.4.cloned.1.call-start = ((), (), s32[]{:S(2)}) async-start(), calls=%async_computation.2 | async-start | bytes 4423680 | tf_op jit(solution)/shard_map/all_gather | solution.py:662
  267.6 20.4 %collective-permute-start.65 = (bf16[512,384]{1,0:T(8,128)(2,1)}, bf16[512,384]{1,0:T(8,128)(2,1)S(1)}, u32[]{:S(2)}, u32[]{:S(2)}) collective-permute-start(bf16[512,384]{1,0:T(8,128)(2,1)} %copy-done.34), channel_id=1, source_target_pairs={{0,4},{4,0},{8,12},{12,8},{16,20},{20,16},{24,28},{28,24},{1,5},{5... | collective-permute-start | bytes 1179656 | tf_op jit(solution)/shard_map/ppermute | solution.py:441
  300.1 82.1 %collective-permute-start.50 = (bf16[4,256,768]{2,1,0:T(8,128)(2,1)}, bf16[4,256,768]{2,1,0:T(8,128)(2,1)S(1)}, u32[]{:S(2)}, u32[]{:S(2)}) collective-permute-start(bf16[4,256,768]{2,1,0:T(8,128)(2,1)} %get-tuple-element.137), channel_id=1, source_target_pairs={{0,4},{4,0},{8,12},{12,8},{16,20},{20,16},{24,28},{28,24},{1,5},{5... | collective-permute-start | bytes 4718600 | tf_op jit(solution)/shard_map/ppermute | solution.py:441
  350.5 31.1 %collective-permute-start.75 = (bf16[208,768]{1,0:T(8,128)(2,1)S(1)}, bf16[208,768]{1,0:T(8,128)(2,1)S(1)}, u32[]{:S(2)}, u32[]{:S(2)}) collective-permute-start(bf16[208,768]{1,0:T(8,128)(2,1)S(1)} %order.3.refs_1_), channel_id=1, source_target_pairs={{0,4},{4,0},{8,12},{12,8},{16,20},{20,16},{24,28},{28,24},{1,5},{5... | collective-permute-start | bytes 958472 | tf_op jit(solution)/shard_map/ppermute | solution.py:441
  383.7 20.7 %collective-permute-start.53 = (bf16[256,768]{1,0:T(8,128)(2,1)S(1)}, bf16[256,768]{1,0:T(8,128)(2,1)S(1)}, u32[]{:S(2)}, u32[]{:S(2)}) collective-permute-start(bf16[256,768]{1,0:T(8,128)(2,1)S(1)} %get-tuple-element.179), channel_id=1, source_target_pairs={{0,24},{4,28},{8,16},{12,20},{16,8},{20,12},{24,0},{28,4},{1,25},{... | collective-permute-start | bytes 1179656 | tf_op jit(solution)/shard_map/ppermute | solution.py:444
  386.1 19.7 %collective-permute-start.52 = (bf16[256,768]{1,0:T(8,128)(2,1)S(1)}, bf16[256,768]{1,0:T(8,128)(2,1)S(1)}, u32[]{:S(2)}, u32[]{:S(2)}) collective-permute-start(bf16[256,768]{1,0:T(8,128)(2,1)S(1)} %get-tuple-element.180), channel_id=1, source_target_pairs={{0,16},{4,20},{8,24},{12,28},{16,0},{20,4},{24,8},{28,12},{1,17},{... | collective-permute-start | bytes 1179656 | tf_op jit(solution)/shard_map/ppermute | solution.py:444
  (156 other events, 1654.8 us)
Sparse Core Ops, SparseCore 0:
  26.5 57.0 all-gather.5
  227.5 40.1 reduce-scatter.1
  269.5 45.0 all-gather.3
where the time goes:
time: 429 us; the launch traced here: 421 us
  waiting for transfers between devices  179 us (42%)
  starting transfers between devices  98.3 us (23%)
  Pallas kernels  65.6 us (15%)
  local copies, waits for them, and re-layouts  35.6 us (8%)
  other arithmetic  26.5 us (6%)
  between operations  15.6 us (4%)
    ppermute x33, waiting for transfers between devices, chip_swap(): return lax.ppermute(x, 'dp', [(i, i ^ 2 * m) for i in range(ndp)])  88.1 us
    pallas_call x27, Pallas kernels, run(): pl.pallas_call(wrapped, out_shape=[jax.ShapeDtypeStruct(s, t) for s, t in...  65.6 us
    ppermute x33, starting transfers between devices, z_rot(): return lax.ppermute(x, 'freq', [(i, (i + k) % nz) for i in range(nz)])  49.8 us
    ppermute x33, waiting for transfers between devices, z_rot(): return lax.ppermute(x, 'freq', [(i, (i + k) % nz) for i in range(nz)])  47.1 us
    ppermute x33, starting transfers between devices, chip_swap(): return lax.ppermute(x, 'dp', [(i, i ^ 2 * m) for i in range(ndp)])  45.7 us
    reduce_scatter x1, waiting for transfers between devices, body(): lax.psum_scatter(mlp_grads, 'freq', scatter_dimension=0, tiled=False)  40.2 us
    unnamed x189, local copies, waits for them, and re-layouts  18.3 us
  transfers between devices with their start and end apart: 89, of which 38 were waited for; matrix products, arithmetic and copies ran while one was open for 11% of the time, Pallas kernels for 12%

commit v1 on v0

v1 whole, which is shorter than its diff:
```python
import functools
import math

import jax
import jax.numpy as jnp
import numpy as np
from jax import lax
from jax.experimental import pallas as pl
from jax.experimental.pallas import tpu as pltpu
from jax.sharding import PartitionSpec as P

SHORT_LENGTH = 128
EPSILON = 1e-05
BF = jnp.bfloat16
F32 = jnp.float32
GROUP = 8
RIDE = 16
COSTS = {
    "project": 20,
    "fold": 20,
    "mix": 15,
    "second_norm": 4,
    "feed": 5,
    "feed_place": 3,
    "down": 4,
    "feed_weights": 5,
    "second_norm_back": 12,
    "mix_back": 5,
    "fold_back": 20,
    "late_weights": 15,
    "first_grad": 4,
    "first_norm_back": 3,
    "late_share": 22,
    "late_sum": 20,
    "gather": 15,
    "last": 6,
    "feed_order": 4,
}
GELU_A = math.sqrt(2.0 / math.pi)
GELU_B = 0.044715


def cosine_table(length):
    freq = np.arange(length)[:, None]
    posit = np.arange(length)[None, :]
    phase = (2 * posit + 1) * freq % (4 * length)
    weight = np.where(freq == 0, 1.0, 2.0) / length
    return (np.cos(phase * (math.pi / (2 * length))) * np.sqrt(weight)).astype(np.float32)


def dot(a, b):
    return lax.dot_general(a, b, (((1,), (0,)), ((), ())), preferred_element_type=F32)


def dot_nt(a, b):
    return lax.dot_general(a, b, (((1,), (1,)), ((), ())), preferred_element_type=F32)


def dot_tn(a, b):
    return lax.dot_general(a, b, (((0,), (0,)), ((), ())), preferred_element_type=F32)


def norm_parts(values):
    center = values - jnp.mean(values, axis=-1, keepdims=True)
    spread = jnp.mean(center * center, axis=-1, keepdims=True)
    inv = lax.rsqrt(spread + EPSILON)
    return center * inv, inv


def norm_pull(hat, inv, gain, grad):
    scaled = grad * gain
    mean_one = jnp.mean(scaled, axis=-1, keepdims=True)
    mean_two = jnp.mean(scaled * hat, axis=-1, keepdims=True)
    return inv * (scaled - mean_one - hat * mean_two), jnp.sum(grad * hat, axis=0, keepdims=True)


def pick(stacked, index):
    return lax.dynamic_index_in_dim(stacked, index, axis=0, keepdims=False)


def run(kernel, name, outs, where, ins, scratch=(), after=()):
    after = [x for x in after if x is not None]
    n_in, n_after = len(ins), len(after)

    def wrapped(*refs):
        kernel(*refs[: 1 + n_in], *refs[1 + n_in + n_after :])

    size = sum(x.size * x.dtype.itemsize for x in ins)
    size += sum(math.prod(s) * jnp.dtype(t).itemsize for s, t in outs)
    return pl.pallas_call(
        wrapped,
        out_shape=[jax.ShapeDtypeStruct(s, t) for s, t in outs],
        in_specs=[pl.BlockSpec(memory_space=pltpu.SMEM)]
        + [
            pl.BlockSpec(memory_space=pltpu.SMEM if x.dtype == jnp.int32 else pltpu.VMEM)
            for x in ins
        ]
        + [pl.BlockSpec(memory_space=pl.ANY)] * n_after,
        out_specs=[pl.BlockSpec(memory_space=pltpu.VMEM)] * len(outs),
        scratch_shapes=list(scratch),
        compiler_params=pltpu.CompilerParams(vmem_limit_bytes=50 * 2**20),
        cost_estimate=pl.CostEstimate(
            flops=int(COSTS.get(name, 1) * 1.15e9), bytes_accessed=int(size), transcendentals=0
        ),
        name=name,
    )(where, *ins, *after)


def rows_at(index, size):
    return pl.ds(pl.multiple_of(index * size, 16), size)


def feed_pick_kernel(where, w_gate_up, w_down, out):
    z, chip, core = where[0], where[1], where[2]
    rows, columns = w_gate_up.shape
    hidden = columns // 2
    per_z = w_down.shape[0]
    chunk = per_z // 6
    member = 2 * chip + core
    for side in range(2):
        for i in range(3):
            zz = i + (i >= chip).astype(jnp.int32)
            c = jnp.where(member < 2 * zz, member, member - 2)
            start = pl.multiple_of(side * hidden + zz * per_z + c * chunk, 128)
            to = (side * 3 + i) * chunk
            out[pl.ds(0, rows), to : to + chunk] = w_gate_up[:, pl.ds(start, chunk)]
    c = jnp.clip(jnp.where(member < 2 * z, member, member - 2), 0, 5)
    out[pl.ds(rows, chunk), :] = w_down[rows_at(c, chunk), :]


def hand_on_kernel(where, n1, n2, n3, in_stack, out_stack):
    wide = in_stack.shape[2]
    for k, near in enumerate((n1, n2, n3)):
        in_stack[k] = near[:, :wide]
        out_stack[k] = near[:, wide:]


def project_kernel(where, marks_own, marks_other, na, nb, local, n1, n2, n3, c1, c2, c3, out_near, cot_in, long_in, short_in, w, outer, left, right, v0, v1, v2, v3, out_stack, cot_low, long, short, vals):
    z, chip = where[0], where[1]
    out_stack[...] = out_near[...]
    cot_low[...] = cot_in[...].astype(BF)
    rows = local.shape[0]
    quarter = rows // 4
    half = outer.shape[1]
    wide = 3 * half
    owned, part = long_in.shape[0], short_in.shape[0]

    def place_filters(at, piece):
        a, b = owned // 4, part // 4
        long[pl.ds(pl.multiple_of(at * a, 8), a), :] = piece[:a]
        short[pl.ds(pl.multiple_of(at * b, 8), b), :] = piece[a : a + b]

    w[rows_at(z, rows), :] = local[...]
    long[rows_at(z, owned), :] = long_in[...].astype(F32)
    short[rows_at(z, part), :] = short_in[...].astype(F32)
    for k, near in ((1, n1), (2, n2), (3, n3)):
        base = ((z - k) & 3) * 4
        w[rows_at(base + chip, quarter), :] = near[:, :wide]
        place_filters(base + chip, near[:, wide : wide + half].astype(F32))
        for m, far in ((1, c1), (2, c2), (3, c3)):
            w[rows_at(base + (chip ^ m), quarter), :] = far[k - 1, :, :wide]
            place_filters(base + (chip ^ m), far[k - 1, :, wide:].astype(F32))
    count = na.shape[0]
    place = lax.broadcasted_iota(jnp.int32, (owned, half), 0)
    for i, (tokens, marks) in enumerate(((na, marks_own), (nb, marks_other))):
        at = pl.ds(i * count, count)
        full = dot(tokens[...], w[...])
        a, b, c = full[:, :half], full[:, half : 2 * half], full[:, 2 * half :]
        outer[at, :] = a
        left[at, :] = b
        right[at, :] = c
        for s in range(count // owned):
            valid = valid_rows(marks, s, z, owned)
            low = slice(s * owned, (s + 1) * owned)
            vals[pl.ds(i * count + s * owned, owned), :] = jnp.where(
                place < valid, b[low] * c[low], 0.0
            ).astype(BF)
    for k, out in enumerate((v0, v1, v2, v3)):
        out[...] = vals[rows_at((z + k) & 3, owned), :]


def valid_rows(marks, s, z, owned):
    total = marks[s, 1] + marks[s, 2] + marks[s, 3] + marks[s, 4]
    return jnp.where(marks[s, 0] == 1, marks[s, 1 + z], total - owned * z)


def neighbours(x, short, length):
    place = lax.broadcasted_iota(jnp.int32, x.shape, 0)
    starts = (place == 0) | (short & (place % SHORT_LENGTH == 0))
    ends = (place == length - 1) | (short & (place % SHORT_LENGTH == SHORT_LENGTH - 1))
    earlier = jnp.where(starts, 0.0, pltpu.roll(x, 1, 0))
    later = jnp.where(ends, 0.0, pltpu.roll(x, length - 1, 0))
    return earlier, later


def fold_kernel(where, v0, r1, r2, r3, long, short_base, table, flipped, gain, taps, vals, spectrum, cond_spec, base, o0, o1, o2, o3, triple, filtered, conv):
    z, short = where[0], where[3] == 1
    owned, half = v0.shape
    length = vals.shape[0]
    for i in range(length // SHORT_LENGTH):
        at = pl.ds(i * SHORT_LENGTH, SHORT_LENGTH)
        base[at, :] = jnp.where(short, short_base[...], long[at, :])
    for k, piece in enumerate((v0, r1, r2, r3)):
        vals[rows_at((z - k) & 3, owned), :] = piece[...]
    wide = vals[...].astype(F32)
    before, after = neighbours(wide, short, length)
    cond = taps[0:1, :] * before + taps[1:2, :] * wide + taps[2:3, :] * after
    high = cond.astype(BF)
    triple[:, :half] = vals[...]
    triple[:, half : 2 * half] = high
    triple[:, 2 * half :] = (cond - high.astype(F32)).astype(BF)
    step = length // 2
    for i in range(2):
        at = pl.ds(i * step, step)
        folded = dot(table[at, :], triple[...])
        spec = folded[:, :half]
        cspec = folded[:, half : 2 * half] + folded[:, 2 * half :]
        spectrum[at, :] = spec
        cond_spec[at, :] = cspec
        kern = base[at, :] + gain[...] * (jnp.sqrt(cspec * cspec + 1.0) - 1.0)
        filtered[at, :] = (kern * spec).astype(BF)
    conv[...] = dot(flipped[...], filtered[...]).astype(BF)
    for k, out in enumerate((o0, o1, o2, o3)):
        out[...] = conv[rows_at((z + k) & 3, owned), :]


def out_rows_kernel(where, mlp_in, local, near_all, c1, c2, c3, keep, send, mlp_all, whole):
    z, chip, core = where[0], where[1], where[2]
    rows, half = local.shape
    mlp_all[...] = mlp_in[...]
    quarter = rows // 4
    whole[rows_at(z, rows), :] = local[...]
    for k in (1, 2, 3):
        base = ((z - k) & 3) * 4
        whole[rows_at(base + chip, quarter), :] = near_all[k - 1]
        for m, far in ((1, c1), (2, c2), (3, c3)):
            whole[rows_at(base + (chip ^ m), quarter), :] = far[k - 1]
    keep[...] = whole[rows_at(core, half), :]
    send[...] = whole[rows_at(1 - core, half), :]


def mix_kernel(where, outer, c0, r1, r2, r3, w_keep, w_came, conv, mixed, own, other, w_rows):
    z, core = where[0], where[2]
    half = outer.shape[1]
    w_rows[:, :half] = jnp.where(core == 0, w_keep[...], w_came[...])
    w_rows[:, half:] = jnp.where(core == 0, w_came[...], w_keep[...])
    owned = c0.shape[0]
    for k, piece in enumerate((c0, r1, r2, r3)):
        conv[rows_at((z - k) & 3, owned), :] = piece[...]
    mixed[...] = (outer[...] * conv[...].astype(F32)).astype(BF)
    count = own.shape[0]
    own[...] = dot(mixed[pl.ds(0, count), :], w_rows[...])
    other[...] = dot(mixed[pl.ds(count, count), :], w_rows[...]).astype(BF)


def second_kernel(where, x, own, came, gain, residual, normed):
    total = x[...] + own[...] + came[...].astype(F32)
    residual[...] = total
    hat, _ = norm_parts(total)
    normed[...] = (hat * gain[...]).astype(BF)


def feed_place_kernel(where, own, other, w_gu, w_dn):
    chip = where[1]
    rows = w_gu.shape[1] // 4
    chunk = own.shape[1] - rows
    for p, part in enumerate((own, other)):
        for i in range(4):
            w_gu[p, pl.ds(i * rows, rows), :] = part[i, pl.ds(0, rows), :]
        for i in range(3):
            at = i + (i >= chip).astype(jnp.int32)
            w_dn[p, pl.ds(i * chunk, chunk), :] = part[at, pl.ds(rows, chunk), :]


def feed_kernel(where, second, cot, w_gu, w_dn, act, grads, out):
    half = w_dn.shape[1]
    width = second.shape[1]
    total = None
    for p in range(2):
        gate_up = dot(second[...], w_gu[p])
        gate, upward = gate_up[:, :half], gate_up[:, half:]
        grad_act = dot_nt(cot[...], w_dn[p])
        square = gate * gate
        tanh = jnp.tanh(GELU_A * gate * (1.0 + GELU_B * square))
        cdf = 0.5 * (1.0 + tanh)
        unit = gate * cdf
        slope = cdf + 0.5 * gate * (1.0 - tanh * tanh) * (GELU_A * (1.0 + 3.0 * GELU_B * square))
        act[:, p * half : (p + 1) * half] = (unit * upward).astype(BF)
        grads[:, p * width : p * width + half] = (grad_act * upward * slope).astype(BF)
        grads[:, p * width + half : (p + 1) * width] = (grad_act * unit).astype(BF)
        part = dot_nt(grads[:, p * width : (p + 1) * width], w_gu[p])
        total = part if total is None else total + part
    out[...] = total.astype(out.dtype)


def down_kernel(where, a0, a1, a2, a3, w_dn, out):
    chip = where[1]
    half = w_dn.shape[1]
    for m, act in enumerate((a0, a1, a2, a3)):
        total = dot(act[:, :half], w_dn[0]) + dot(act[:, half:], w_dn[1])
        out[chip ^ m] = total.astype(BF)


def feed_weight_kernel(p, where, a0, a1, a2, a3, g0, g1, g2, g3, s0, s1, s2, s3, c0, c1, c2, c3, *rest):
    came, (out, acts, grads, seconds, cots) = rest[:-5], rest[-5:]
    chip = where[1]
    count, width = s0.shape
    half = width // 2
    for m, (a, g, s, c) in enumerate(
        ((a0, g0, s0, c0), (a1, g1, s1, c1), (a2, g2, s2, c2), (a3, g3, s3, c3))
    ):
        at = pl.ds(m * count, count)
        acts[at, :] = a[:, p * half : (p + 1) * half]
        grads[at, :] = g[:, p * width : (p + 1) * width]
        seconds[at, :] = s[...]
        cots[at, :] = c[...]
    nz, piece, _ = out.shape
    chunk = half // 3
    rows = piece - chunk

    def put(i, start, value):
        place = pl.ds(start, value.shape[0])
        if came:
            value = value + came[0][i, place, :].astype(F32)
        out[i, place, :] = value.astype(BF)

    total = dot_tn(seconds[...], grads[...])
    for i in range(nz):
        put(i, 0, total[i * rows : (i + 1) * rows])
    down = dot_tn(acts[...], cots[...])
    out[chip, pl.ds(rows, chunk), :] = jnp.zeros((chunk, width), BF)
    for i in range(3):
        to = i + (i >= chip).astype(jnp.int32)
        put(to, rows, down[i * chunk : (i + 1) * chunk])


def copy_kernel(where, a, out):
    out[...] = a[...]


def layer_out_kernel(where, residual, rest, out):
    total = residual[...] + rest[...].astype(F32)
    owned = out.shape[0]
    for i in range(out.shape[1]):
        out[:, i, :] = total[i * owned : (i + 1) * owned]


def second_back_kernel(where, residual, gain, cot, own, r1, r2, r3, grad_residual, low, grad_gain):
    grad = own[...] + r1[...].astype(F32) + r2[...].astype(F32) + r3[...].astype(F32)
    hat, inv = norm_parts(residual[...])
    pulled, grad_gain[...] = norm_pull(hat, inv, gain[...], grad)
    total = cot[...] + pulled
    grad_residual[...] = total
    low[...] = total.astype(BF)


def mix_back_kernel(where, ga, gb, w_rows, outer, conv, na, nb, mixed, other_mixed, grad_outer, o0, o1, o2, o3, p0, p1, p2, p3, grad_conv, whole):
    z, chip, core = where[0], where[1], where[2]
    count = ga.shape[0]
    half = outer.shape[1]
    for i, grad in enumerate((ga, gb)):
        at = pl.ds(i * count, count)
        grad_mixed = dot_nt(grad[...], w_rows[...])
        grad_outer[at, :] = (grad_mixed * conv[at, :].astype(F32)).astype(BF)
        grad_conv[at, :] = (grad_mixed * outer[at, :]).astype(BF)
    owned = o0.shape[0]
    for k, out in enumerate((o0, o1, o2, o3)):
        out[...] = grad_conv[rows_at((z + k) & 3, owned), :]
    total = dot_tn(na[...], grad_outer[pl.ds(0, count), :])
    total = total + dot_tn(nb[...], grad_outer[pl.ds(count, count), :])
    whole[:, :half] = total.astype(BF)
    first = jnp.where(core == 0, ga[:, :half], ga[:, half:])
    second = jnp.where(core == 0, gb[:, :half], gb[:, half:])
    mine = dot_tn(mixed[pl.ds(0, count), :], first) + dot_tn(mixed[pl.ds(count, count), :], second)
    theirs = dot_tn(other_mixed[pl.ds(count, count), :], first)
    theirs = theirs + dot_tn(other_mixed[pl.ds(0, count), :], second)
    whole[rows_at(core, half), half:] = mine.astype(BF)
    whole[rows_at(1 - core, half), half:] = theirs.astype(BF)
    write_pieces(whole, (p0, p1, p2, p3), chip)


def fold_back_kernel(where, g0, r1, r2, r3, table, flipped, spectrum, cond_spec, base, gain, taps, vals, o0, o1, o2, o3, f0, f1, f2, f3, grads, double, filters):
    z, short = where[0], where[3] == 1
    owned, half = g0.shape
    length = vals.shape[0]
    for k, piece in enumerate((g0, r1, r2, r3)):
        grads[rows_at((z - k) & 3, owned), :] = piece[...]
    gf = dot(table[...], grads[...])
    cspec = cond_spec[...]
    root = jnp.sqrt(cspec * cspec + 1.0)
    above = root - 1.0
    grad_base = gf * spectrum[...]
    double[:, :half] = (gf * (base[...] + gain[...] * above)).astype(BF)
    double[:, half:] = (grad_base * gain[...] * (cspec / root)).astype(BF)
    unfolded = dot(flipped[...], double[...])
    grad_cond = unfolded[:, half:]
    wide = vals[...].astype(F32)
    before, after = neighbours(wide, short, length)
    grad_before, grad_after = neighbours(grad_cond, short, length)
    grads[...] = (
        unfolded[:, :half]
        + taps[0:1, :] * grad_after
        + taps[1:2, :] * grad_cond
        + taps[2:3, :] * grad_before
    ).astype(BF)
    for k, out in enumerate((o0, o1, o2, o3)):
        out[...] = grads[rows_at((z + k) & 3, owned), :]
    is_short = jnp.where(short, 1.0, 0.0)
    filters[pl.ds(0, length), :] = (grad_base * (1.0 - is_short)).astype(BF)
    folded = grad_base[:SHORT_LENGTH]
    for i in range(1, length // SHORT_LENGTH):
        folded = folded + grad_base[i * SHORT_LENGTH : (i + 1) * SHORT_LENGTH]
    filters[pl.ds(length, SHORT_LENGTH), :] = (folded * is_short).astype(BF)
    rest = filters.shape[0] - length - SHORT_LENGTH
    small = [
        jnp.sum(grad_base * above, axis=0, keepdims=True),
        jnp.sum(grad_cond * before, axis=0, keepdims=True),
        jnp.sum(grad_cond * wide, axis=0, keepdims=True),
        jnp.sum(grad_cond * after, axis=0, keepdims=True),
        jnp.zeros((rest - 4, half), F32),
    ]
    filters[pl.ds(length + SHORT_LENGTH, rest), :] = jnp.concatenate(small, axis=0).astype(BF)
    size = f0.shape[0]
    for k, out in enumerate((f0, f1, f2, f3)):
        start = ((z + k) & 3) * 2
        out[:, :half] = filters[rows_at(start, size), :]
        out[:, half:] = filters[rows_at(start + 1, size), :]


def write_pieces(whole, outs, chip):
    rows = whole.shape[0] // 4
    quarter = rows // 4
    for m, out in enumerate(outs):
        for i in range(4):
            out[pl.ds(i * quarter, quarter), :] = whole[rows_at(i * 4 + (chip ^ m), quarter), :]


def late_kernel(where, marks_own, marks_other, g0, r1, r2, r3, left, right, na, nb, late, p0, p1, p2, p3, grads, whole):
    z, chip = where[0], where[1]
    owned, half = g0.shape
    for k, piece in enumerate((g0, r1, r2, r3)):
        grads[rows_at((z - k) & 3, owned), :] = piece[...].astype(F32)
    count = na.shape[0]
    place = lax.broadcasted_iota(jnp.int32, (owned, half), 0)
    for i, marks in enumerate((marks_own, marks_other)):
        for s in range(count // owned):
            at = pl.ds(i * count + s * owned, owned)
            grad = jnp.where(place < valid_rows(marks, s, z, owned), grads[at, :], 0.0)
            late[at, :half] = (grad * right[at, :]).astype(BF)
            late[at, half:] = (grad * left[at, :]).astype(BF)
    total = dot_tn(na[...], late[pl.ds(0, count), :]) + dot_tn(nb[...], late[pl.ds(count, count), :])
    whole[...] = total.astype(BF)
    write_pieces(whole, (p0, p1, p2, p3), chip)


def first_grad_kernel(where, grad_outer, late, w, own, other):
    half = grad_outer.shape[1]
    count = own.shape[0]
    for i, out in enumerate((own, other)):
        at = pl.ds(i * count, count)
        total = dot_nt(grad_outer[at, :], w[:, :half]) + dot_nt(late[at, :], w[:, half:])
        out[...] = total.astype(out.dtype)


def first_back_kernel(where, x, gain, grad_residual, own, came, grad_inputs, grad_gain):
    grad = own[...] + came[...].astype(F32)
    hat, inv = norm_parts(x[...])
    pulled, grad_gain[...] = norm_pull(hat, inv, gain[...], grad)
    total = grad_residual[...] + pulled
    owned = grad_inputs.shape[0]
    for i in range(grad_inputs.shape[1]):
        grad_inputs[:, i, :] = total[i * owned : (i + 1) * owned]


def added(pieces):
    total = pieces[0][...].astype(F32)
    for piece in pieces[1:]:
        total = total + piece[...].astype(F32)
    return total


def ridden(row, width):
    first = lax.broadcasted_iota(jnp.int32, (RIDE, width), 0) == 0
    return jnp.where(first, jnp.broadcast_to(row, (RIDE, width)), 0.0).astype(BF)


def early_share_kernel(where, p0, r1, r2, r3, ride, f0, f1, f2, f3, o0, o1, o2, o3, total):
    z = where[0]
    total[...] = added((p0, r1, r2, r3)).astype(BF)
    quarter = p0.shape[0] // 4
    extra = ridden(ride[...], p0.shape[1])
    for k, (filt, out) in enumerate(((f0, o0), (f1, o1), (f2, o2), (f3, o3))):
        out[pl.ds(0, quarter), :] = total[rows_at((z + k) & 3, quarter), :]
        out[pl.ds(quarter, RIDE), :] = extra
        out[pl.ds(quarter + RIDE, filt.shape[0]), :] = filt[...]


def late_share_kernel(where, p0, r1, r2, r3, ride, e0, e1, e2, e3, o0, o1, o2, o3, early, total):
    z = where[0]
    total[...] = added((p0, r1, r2, r3)).astype(BF)
    quarter = p0.shape[0] // 4
    extra = ridden(ride[...], p0.shape[1])
    for k, out in enumerate((o0, o1, o2, o3)):
        out[pl.ds(0, quarter), :] = total[rows_at((z + k) & 3, quarter), :]
        out[pl.ds(quarter, RIDE), :] = extra
    early[...] = added((e0, e1, e2, e3)).astype(BF)


def in_order(where, pieces, out, start):
    chip = where[1]
    quarter = pieces[0].shape[0] - RIDE
    width = pieces[0].shape[1]
    riding = jnp.zeros((1, width), F32)
    for m, piece in enumerate(pieces):
        out[rows_at(start // quarter + (chip ^ m), quarter), :] = piece[pl.ds(0, quarter), :]
        riding = riding + piece[pl.ds(quarter, RIDE), :].astype(F32)[0:1]
    out[pl.ds(start + 4 * quarter, RIDE), :] = ridden(riding, width)


def late_sum_kernel(where, s0, r1, r2, r3, e0, e1, e2, e3, piece, filt, early):
    piece[...] = added((s0, r1, r2, r3)).astype(BF)
    size = s0.shape[0]
    filt[...] = added([e.at[pl.ds(size, filt.shape[0])] for e in (e0, e1, e2, e3)]).astype(BF)
    in_order(where, [e.at[pl.ds(0, size)] for e in (e0, e1, e2, e3)], early, 0)


def gather_kernel(where, s0, r1, r2, r3, f0, f1, f2, f3, early, out):
    z = where[0]
    in_order(where, (s0, r1, r2, r3), out, 0)
    size = early.shape[0]
    out[pl.ds(size, size), :] = early[...]
    step = f0.shape[0]
    for k, piece in enumerate((f0, f1, f2, f3)):
        out[pl.ds(pl.multiple_of(2 * size + ((z - k) & 3) * step, 16), step), :] = piece[...]


def feed_order_kernel(where, shares, gate_up, down):
    z = where[0]
    rows = gate_up.shape[0]
    chunk = shares.shape[1] - rows
    per_z = 6 * chunk
    for side in range(2):
        for zz in range(4):
            for c in range(6):
                mm = c if c < 2 * zz else c + 2
                at = (side * 3 + zz - (zz > mm // 2)) * chunk
                to = side * 4 * per_z + zz * per_z + c * chunk
                gate_up[:, to : to + chunk] = shares[mm, :rows, at : at + chunk].astype(F32)
    for c in range(6):
        mm = c + 2 * (c >= 2 * z).astype(jnp.int32)
        down[pl.ds(c * chunk, chunk), :] = shares[mm, pl.ds(rows, chunk), :].astype(F32)


def last_kernel(where, own, other, w_in, w_out, long, short, gain, taps, norm_one, norm_two):
    core = where[2]
    rows = w_in.shape[0]
    width = w_out.shape[1]
    half = width // 2
    size = rows + RIDE

    def write(out, to, a, b):
        a, b = a.astype(F32), b.astype(F32)
        out[:, to : to + half] = jnp.where(core == 0, a, b)
        out[:, to + half : to + width] = jnp.where(core == 0, b, a)

    for start, at, to, out in (
        (size, 0, 0, w_in),
        (0, 0, width, w_in),
        (0, half, 2 * width, w_in),
        (size, half, 0, w_out),
    ):
        place = (pl.ds(start, rows), slice(at, at + half))
        write(out, to, own[place], other[place])
    for start, out in ((0, norm_one), (size, norm_two)):
        place = pl.ds(start + rows, RIDE)
        out[...] = (own[place, :].astype(F32) + other[place, :].astype(F32))[0:1]
    fold = (own.shape[0] - 2 * size) // 4
    length, part = long.shape[0], short.shape[0]

    def filter_rows(ref, start, count):
        got = []
        while count:
            block, inside = start // fold, start % fold
            step = min(count, fold - inside)
            place = pl.ds(2 * size + block // 2 * fold + inside, step)
            got.append(ref[place, half:] if block % 2 else ref[place, :half])
            start, count = start + step, count - step
        return jnp.concatenate(got, axis=0) if len(got) > 1 else got[0]

    for i in range(0, length, SHORT_LENGTH):
        a, b = filter_rows(own, i, SHORT_LENGTH), filter_rows(other, i, SHORT_LENGTH)
        write(long.at[pl.ds(i, SHORT_LENGTH)], 0, a, b)
    write(short, 0, filter_rows(own, length, part), filter_rows(other, length, part))
    a, b = filter_rows(own, length + part, 16), filter_rows(other, length + part, 16)
    write(gain, 0, a[0:1], b[0:1])
    write(taps, 0, a[1:4], b[1:4])


def body(
    inputs,
    cotangent,
    group,
    lens,
    norm1_gain,
    w_in,
    kernel_long,
    kernel_short,
    conv_weight,
    cond_gain,
    w_out,
    norm2_gain,
    w_gate_up,
    w_down,
):
    nz = lax.axis_size("freq")
    ndp = lax.axis_size("dp")
    z = lax.axis_index("freq")
    d = lax.axis_index("dp")
    core = d % 2
    chip = (d // 2) % 4
    member = d % GROUP
    owned, slots, width = inputs.shape
    half = width // 2
    length = owned * nz
    tokens = owned * slots
    rows = w_in.shape[0]
    quarter = rows // 4
    others = ndp // GROUP
    blocks = [[g * GROUP + i for i in range(GROUP)] for g in range(others)]
    same_core = [[g * GROUP + 2 * i + c for i in range(4)] for g in range(others) for c in range(2)]
    across = [[i + GROUP * g for g in range(others)] for i in range(GROUP)]

    def core_swap(x):
        return lax.ppermute(x, "dp", [(i, i ^ 1) for i in range(ndp)])

    def chip_swap(x, m):
        return lax.ppermute(x, "dp", [(i, i ^ (2 * m)) for i in range(ndp)])

    def z_rot(x, k):
        return lax.ppermute(x, "freq", [(i, (i + k) % nz) for i in range(nz)])

    def mine(x, axis=-1):
        low, high = jnp.split(x, 2, axis=axis)
        return jnp.where(core == 0, low, high)

    def theirs(x, axis=-1):
        low, high = jnp.split(x, 2, axis=axis)
        return jnp.where(core == 0, high, low)

    def joined(own, other, axis=-1):
        return jnp.where(
            core == 0,
            jnp.concatenate([own, other], axis=axis),
            jnp.concatenate([other, own], axis=axis),
        )

    def from_z(rel):
        stacked = jnp.stack(rel)
        return jnp.concatenate([pick(stacked, (z - i) % nz) for i in range(nz)], axis=0)

    def z_swap(pieces):
        return [pieces[0]] + [z_rot(pieces[k], k) for k in range(1, nz)]

    def over_groups(x):
        if others > 1:
            return lax.psum(x, "dp", axis_index_groups=across)
        return x

    def in_cols(x):
        return jnp.concatenate([mine(x[:, i * width : (i + 1) * width]) for i in range(3)], axis=1)

    where = jnp.stack([z, chip, core, z]).astype(jnp.int32)
    start = chip * quarter
    part = kernel_short.shape[0]
    long_half, short_half = mine(kernel_long), mine(kernel_short)
    filt_near = jnp.concatenate(
        [
            lax.dynamic_slice_in_dim(long_half, chip * (owned // 4), owned // 4, axis=0),
            lax.dynamic_slice_in_dim(short_half, chip * (part // 4), part // 4, axis=0),
            jnp.zeros((quarter - (owned + part) // 4, half), BF),
        ],
        axis=0,
    )
    near = jnp.concatenate(
        [
            in_cols(lax.dynamic_slice_in_dim(w_in, start, quarter, axis=0)),
            filt_near,
            mine(lax.dynamic_slice_in_dim(w_out, start, quarter, axis=0)),
        ],
        axis=1,
    )
    both_near = [z_rot(near, k) for k in range(1, nz)]

    hidden = w_down.shape[0] * nz
    per_z = w_down.shape[0]
    chunk = per_z // 6
    taken = rows + chunk

    x_own = jnp.swapaxes(inputs, 0, 1).reshape(tokens, width)
    cot_own = jnp.swapaxes(cotangent, 0, 1).reshape(tokens, width)

    marks = jnp.concatenate([group[:, None], lens], axis=1).astype(jnp.int32)
    marks_other = core_swap(marks)
    group_all = jnp.concatenate([marks[:, 0], marks_other[:, 0]])
    slot_group = pick(group_all, z)
    spot = jnp.stack([z, chip, core, slot_group]).astype(jnp.int32)

    repeat = length // SHORT_LENGTH
    long_table = cosine_table(length)
    short_table = np.kron(np.eye(repeat), cosine_table(SHORT_LENGTH)).astype(np.float32)
    is_short = slot_group == 1
    table = jnp.where(is_short, jnp.asarray(short_table, BF), jnp.asarray(long_table, BF))
    flipped = jnp.where(is_short, jnp.asarray(short_table.T, BF), jnp.asarray(long_table.T, BF))
    gain_half = mine(cond_gain)[None]
    taps = mine(conv_weight)
    gain_one = norm1_gain[None]
    gain_two = norm2_gain[None]

    hat_one, _ = norm_parts(x_own)
    normed = (hat_one * gain_one).astype(BF)
    normed_other = core_swap(normed)
    piece = ((owned, half), BF)
    many = 2 * tokens
    out_local = mine(w_out)
    in_stack, out_near = run(
        hand_on_kernel,
        "hand_on",
        [((3, quarter, 4 * half), BF), ((3, quarter, half), BF)],
        where,
        both_near,
    )
    mlp_piece = run(
        feed_pick_kernel,
        "feed_pick",
        [((taken, width), BF)],
        where,
        [w_gate_up, w_down],
        after=(in_stack,),
    )[0]
    mlp_got = lax.all_gather(mlp_piece, "freq", axis=0)
    in_far = [chip_swap(in_stack, m) for m in (1, 2, 3)]
    w_in_half, outer, left, right, s0, s1, s2, s3, out_stack, cot_low, long, short = run(
        project_kernel,
        "project",
        [((width, 3 * half), BF)]
        + [((many, half), F32)] * 3
        + [piece] * 4
        + [((3, quarter, half), BF), ((tokens, width), BF)]
        + [((length, half), F32), ((part * nz, half), F32)],
        where,
        [
            marks,
            marks_other,
            normed,
            normed_other,
            in_cols(w_in),
            *both_near,
            *in_far,
            out_near,
            cot_own,
            long_half,
            short_half,
        ],
        [pltpu.VMEM((many, half), BF)],
    )
    came = z_swap([s0, s1, s2, s3])
    out_far = [chip_swap(out_stack, m) for m in (1, 2, 3)]
    cots = [cot_low] + [chip_swap(cot_low, m) for m in (1, 2)]
    vals, spectrum, cond_spec, base, *sends = run(
        fold_kernel,
        "fold",
        [((length, half), BF)] + [((length, half), F32)] * 3 + [piece] * 4,
        spot,
        [*came, long, short, table, flipped, gain_half, taps],
        [
            pltpu.VMEM((length, 3 * half), BF),
            pltpu.VMEM((length, half), BF),
            pltpu.VMEM((length, half), BF),
        ],
        after=(*cots[1:], *out_far),
    )
    came = z_swap(sends)
    cot_far = run(copy_kernel, "cot_far", [(cot_low.shape, BF)], where, [cot_low], after=(vals,))[0]
    cots.append(chip_swap(cot_far, 3))
    w_keep, w_send, mlp_all = run(
        out_rows_kernel,
        "out_rows",
        [((half, half), BF)] * 2 + [((nz, taken, width), BF)],
        where,
        [mlp_got, out_local, out_near, *out_far],
        [pltpu.VMEM((width, half), BF)],
        after=(vals,),
    )
    w_gu, w_dn = run(
        feed_place_kernel,
        "feed_place",
        [((2, width, width), BF), ((2, half, width), BF)],
        where,
        [mlp_all, core_swap(mlp_all)],
    )
    conv, mixed, part_own, part_other, w_out_rows = run(
        mix_kernel,
        "mix",
        [((many, half), BF)] * 2
        + [((tokens, width), F32), ((tokens, width), BF), ((half, width), BF)],
        where,
        [outer, *came, w_keep, core_swap(w_send)],
        after=(w_gu, cots[3]),
    )
    residual, normed_two = run(
        second_kernel,
        "second_norm",
        [((tokens, width), F32), ((tokens, width), BF)],
        where,
        [x_own, part_own, core_swap(part_other), gain_two],
    )

    arrived = [normed_two] + [chip_swap(normed_two, m) for m in (1, 2, 3)]
    acts, grads_gu, sums = [], [], []
    order = ()
    for m in range(4):
        act, grad_gu, part = run(
            feed_kernel,
            "feed",
            [((tokens, width), BF), ((tokens, 2 * width), BF), ((tokens, width), BF if m else F32)],
            where,
            [arrived[m], cots[m], w_gu, w_dn],
            after=order,
        )
        order = (act,)
        acts.append(act)
        grads_gu.append(grad_gu)
        sums.append(part)
    backs = [chip_swap(sums[m], m) for m in (1, 2, 3)]
    partial_out = run(
        down_kernel,
        "down",
        [((4, tokens, width), BF)],
        where,
        [*acts, w_dn],
    )[0]
    down_sum = lax.psum_scatter(
        partial_out, "dp", scatter_dimension=0, axis_index_groups=same_core, tiled=False
    )
    grad_residual, grad_mix, grad_gain_two = run(
        second_back_kernel,
        "second_norm_back",
        [((tokens, width), F32), ((tokens, width), BF), ((1, width), F32)],
        where,
        [residual, gain_two, cot_own, sums[0], *backs],
    )
    grad_mix_other = core_swap(grad_mix)
    grad_outer, s0, s1, s2, s3, *early_parts = run(
        mix_back_kernel,
        "mix_back",
        [((many, half), BF)] + [piece] * 4 + [((rows, width), BF)] * 4,
        where,
        [
            grad_mix,
            grad_mix_other,
            w_out_rows,
            outer,
            conv,
            normed,
            normed_other,
            mixed,
            core_swap(mixed),
        ],
        [pltpu.VMEM((many, half), BF), pltpu.VMEM((width, width), BF)],
    )
    came = z_swap([s0, s1, s2, s3])

    def near_by(piece):
        return [piece] + [chip_swap(piece, m) for m in (1, 2, 3)]

    def exchanged(parts):
        return [parts[0]] + [chip_swap(parts[m], m) for m in (1, 2, 3)]

    early_all = exchanged(early_parts)

    def feed_weights(p, came, after):
        return run(
            functools.partial(feed_weight_kernel, p),
            "feed_weights",
            [((nz, taken, width), BF)],
            where,
            [*acts, *grads_gu, *arrived, *cots, *came],
            [
                pltpu.VMEM((4 * tokens, half), BF),
                pltpu.VMEM((4 * tokens, width), BF),
                pltpu.VMEM((4 * tokens, width), BF),
                pltpu.VMEM((4 * tokens, width), BF),
            ],
            after=after,
        )[0]

    mlp_send = feed_weights(1, [], (grad_outer,))
    mlp_grads = feed_weights(0, [core_swap(mlp_send)], ())
    mlp_share = lax.psum_scatter(mlp_grads, "freq", scatter_dimension=0, tiled=False)

    fill = -(length + SHORT_LENGTH + 4) % (nz * 32)
    size = (length + SHORT_LENGTH + 4 + fill) // nz // 2
    *sends, f0, f1, f2, f3 = run(
        fold_back_kernel,
        "fold_back",
        [piece] * 4 + [((size, width), BF)] * 4,
        spot,
        [*came, table, flipped, spectrum, cond_spec, base, gain_half, taps, vals],
        [
            pltpu.VMEM((length, half), BF),
            pltpu.VMEM((length, 2 * half), BF),
            pltpu.VMEM((2 * size * nz, half), BF),
        ],
        after=early_all[1:],
    )
    came = z_swap(sends)
    pack = quarter + RIDE + size
    early_sends = run(
        early_share_kernel,
        "early_share",
        [((pack, width), BF)] * 4,
        where,
        [*early_all, grad_gain_two, f0, f1, f2, f3],
        [pltpu.VMEM((rows, width), BF)],
    )
    late, *late_parts = run(
        late_kernel,
        "late_weights",
        [((many, width), BF)] + [((rows, width), BF)] * 4,
        where,
        [marks, marks_other, *came, left, right, normed, normed_other],
        [pltpu.VMEM((many, half), F32), pltpu.VMEM((width, width), BF)],
        after=(early_sends[0],),
    )
    late_all = exchanged(late_parts)
    own, other = run(
        first_grad_kernel,
        "first_grad",
        [((tokens, width), F32), ((tokens, width), BF)],
        where,
        [grad_outer, late, w_in_half],
    )
    layer_out = run(
        layer_out_kernel,
        "layer_out",
        [((owned, slots, width), F32)],
        where,
        [residual, down_sum],
        after=(own,),
    )[0]
    grad_inputs, grad_gain_one = run(
        first_back_kernel,
        "first_norm_back",
        [((owned, slots, width), F32), ((1, width), F32)],
        where,
        [x_own, gain_one, grad_residual, own, core_swap(other)],
        after=(layer_out,),
    )
    mlp_sum = lax.all_gather(over_groups(mlp_share), "dp", axis=0, axis_index_groups=blocks)
    *late_sends, early = run(
        late_share_kernel,
        "late_share",
        [((quarter + RIDE, width), BF)] * 4 + [((pack, width), BF)],
        where,
        [*late_all, grad_gain_one, *z_swap(early_sends)],
        [pltpu.VMEM((rows, width), BF)],
    )
    late_piece, filt, early = run(
        late_sum_kernel,
        "late_sum",
        [((quarter + RIDE, width), BF), ((size, width), BF), ((rows + RIDE, width), BF)],
        where,
        [*z_swap(late_sends), *near_by(over_groups(early))],
    )
    gathered = run(
        gather_kernel,
        "gather",
        [((2 * (rows + RIDE) + nz * size, width), BF)],
        where,
        [*near_by(over_groups(late_piece)), *z_swap([filt] * nz), early],
    )[0]
    grad_w_gate_up, grad_w_down = run(
        feed_order_kernel,
        "feed_order",
        [((rows, 2 * hidden), F32), ((per_z, width), F32)],
        where,
        [mlp_sum],
    )
    grad_w_in, grad_w_out, grad_long, grad_short, grad_cond, grad_taps, grad_one, grad_two = run(
        last_kernel,
        "last",
        [
            ((rows, 3 * width), F32),
            ((rows, width), F32),
            ((length, width), F32),
            ((SHORT_LENGTH, width), F32),
            ((1, width), F32),
            ((3, width), F32),
            ((1, width), F32),
            ((1, width), F32),
        ],
        where,
        [gathered, core_swap(gathered)],
    )

    return (
        layer_out,
        grad_inputs,
        grad_one.reshape(width),
        grad_w_in,
        grad_long,
        grad_short,
        grad_taps,
        grad_cond.reshape(width),
        grad_w_out,
        grad_two.reshape(width),
        grad_w_gate_up,
        grad_w_down,
    )


def solution(mesh):
    return jax.shard_map(
        body,
        mesh=mesh,
        in_specs=(
            P("freq", "dp", None),
            P("freq", "dp", None),
            P("dp"),
            P("dp", None),
            P(),
            P("freq", None),
            P("freq", None),
            P("freq", None),
            P(),
            P(),
            P("freq", None),
            P(),
            P("freq", None),
            P("freq", None),
        ),
        out_specs=(
            P("freq", "dp", None),
            P("freq", "dp", None),
            P(),
            P("freq", None),
            P(),
            P(),
            P(),
            P(),
            P("freq", None),
            P(),
            P("freq", None),
            P("freq", None),
        ),
        check_vma=False,
    )
```

time: 429 us -> 342 us (0.80); the launches traced: 421 us -> 340 us
  waiting for transfers between devices: 179 us -> 102 us
  Pallas kernels: 65.6 us -> 85.5 us
  other arithmetic: 26.5 us -> 15.9 us
  starting transfers between devices: 98.3 us -> 90.2 us
    ppermute x33 -> x27, waiting for transfers between devices: 88.1 us -> 48.7 us  [chip_swap(): return lax.ppermute(x, 'dp', [(i, i ^ 2 * m) for i in range(ndp)])]
    reduce_scatter x1, waiting for transfers between devices: 40.2 us -> 15.8 us  [body(): lax.psum_scatter(mlp_grads, 'freq', scatter_dimension=0, tiled=False)]
    pallas_call x27 -> x29, Pallas kernels: 65.6 us -> 85.5 us  [run(): pl.pallas_call(wrapped, out_shape=[jax.ShapeDtypeStruct(s, t) for s, t in...]
    ppermute x33 -> x27, starting transfers between devices: 45.7 us -> 27.8 us  [chip_swap(): return lax.ppermute(x, 'dp', [(i, i ^ 2 * m) for i in range(ndp)])]
    ppermute x33 -> x24, waiting for transfers between devices: 47.1 us -> 32.2 us  [z_rot(): return lax.ppermute(x, 'freq', [(i, (i + k) % nz) for i in range(nz)])]
    ppermute x33 -> x24, starting transfers between devices: 49.8 us -> 60.6 us  [z_rot(): return lax.ppermute(x, 'freq', [(i, (i + k) % nz) for i in range(nz)])]
    unnamed x189 -> x178, local copies, waits for them, and re-layouts: 18.3 us -> 28.9 us
    slice x9 -> x1, local copies, waits for them, and re-layouts: 6.81 us -> 0.11 us  [body(): group_all = jnp.concatenate([marks[:, 0], marks_other[:, 0]])]
  transfers between devices with their start and end apart: 89 -> 65, of which waited for: 38 -> 24; matrix products, arithmetic and copies ran while one was open for 11% -> 3% of each run, Pallas kernels for 12% -> 22%
where the time goes in v1:
time: 342 us; the launch traced here: 340 us
  waiting for transfers between devices  102 us (30%)
  starting transfers between devices  90.2 us (26%)
  Pallas kernels  85.5 us (25%)
  local copies, waits for them, and re-layouts  31.4 us (9%)
  other arithmetic  15.9 us (5%)
  between operations  15.4 us (5%)
    pallas_call x29, Pallas kernels, run(): pl.pallas_call(wrapped, out_shape=[jax.ShapeDtypeStruct(s, t) for s, t in...  85.5 us
    ppermute x24, starting transfers between devices, z_rot(): return lax.ppermute(x, 'freq', [(i, (i + k) % nz) for i in range(nz)])  60.6 us
    ppermute x27, waiting for transfers between devices, chip_swap(): return lax.ppermute(x, 'dp', [(i, i ^ 2 * m) for i in range(ndp)])  48.7 us
    ppermute x24, waiting for transfers between devices, z_rot(): return lax.ppermute(x, 'freq', [(i, (i + k) % nz) for i in range(nz)])  32.2 us
    unnamed x178, local copies, waits for them, and re-layouts  28.9 us
    ppermute x27, starting transfers between devices, chip_swap(): return lax.ppermute(x, 'dp', [(i, i ^ 2 * m) for i in range(ndp)])  27.8 us
    reduce_scatter x1, waiting for transfers between devices, body(): lax.psum_scatter(mlp_grads, 'freq', scatter_dimension=0, tiled=False)  15.8 us
  transfers between devices with their start and end apart: 65, of which 24 were waited for; matrix products, arithmetic and copies ran while one was open for 3% of the time, Pallas kernels for 22%

profile of v1, /device:TPU:0, one launch (start us, length us, event | category | flops | bytes accessed | tf_op | source)
XLA Modules:
  0.0 340.3 jit_solution(13563036147183630900)
XLA Ops:
  42.0 5.9 %collective-permute-done.5.refs_9_ = bf16[3,48,1536]{2,1,0:T(8,128)(2,1)S(1)} collective-permute-done((bf16[3,48,1536]{2,1,0:T(8,128)(2,1)S(1)}, bf16[3,48,1536]{2,1,0:T(8,128)(2,1)S(1)}, u32[]{:S(2)}, u32[]{:S(2)}) %collective-permute-start.5) | collective-permute-done | bytes 442400 | tf_op jit(solution)/shard_map/ppermute | solution.py:637
  47.9 9.6 %collective-permute-done.6.refs_10_ = bf16[3,48,1536]{2,1,0:T(8,128)(2,1)S(1)} collective-permute-done((bf16[3,48,1536]{2,1,0:T(8,128)(2,1)S(1)}, bf16[3,48,1536]{2,1,0:T(8,128)(2,1)S(1)}, u32[]{:S(2)}, u32[]{:S(2)}) %collective-permute-start.6) | collective-permute-done | bytes 442400 | tf_op jit(solution)/shard_map/ppermute | solution.py:637
  60.3 5.1 %project.1 = (bf16[768,1152]{1,0:T(8,128)(2,1)}, f32[512,384]{1,0:T(8,128)}, f32[512,384]{1,0:T(8,128)}, f32[512,384]{1,0:T(8,128)}, bf16[128,384]{1,0:T(8,128)(...) custom-call(s32[4]{0:T(128)S(1)} %pad_add_fusion.1.refs_0_, ...), custom_call_target="tpu_custom_call" | custom-call | flops 23000000512 | bytes 10137680 | tf_op jit(solution)/shard_map/project/pallas_call | solution.py:90
  68.2 4.5 %collective-permute-start.8 = (bf16[128,384]{1,0:T(8,128)(2,1)S(1)}, bf16[128,384]{1,0:T(8,128)(2,1)S(1)}, u32[]{:S(2)}, u32[]{:S(2)}) collective-permute-start(bf16[128,384]{1,0:T(8,128)(2,1)S(1)} %get-tuple-element.113), channel_id=1, source_target_pairs={{0,1},{1,2},{2,3},{3,0},{4,5},{5,6},{6,7},{7,4},{8,9},{9,10},{10,1... | collective-permute-start | bytes 294920 | tf_op jit(solution)/shard_map/ppermute | solution.py:640
  79.9 4.6 %collective-permute-done.9.refs_3_ = bf16[128,384]{1,0:T(8,128)(2,1)S(1)} collective-permute-done((bf16[128,384]{1,0:T(8,128)(2,1)S(1)}, bf16[128,384]{1,0:T(8,128)(2,1)S(1)}, u32[]{:S(2)}, u32[]{:S(2)}) %collective-permute-start.9) | collective-permute-done | bytes 98336 | tf_op jit(solution)/shard_map/ppermute | solution.py:640
  87.5 4.2 %collective-permute-done.14.refs_14_.refs_5_ = bf16[3,48,384]{2,1,0:T(8,128)(2,1)S(1)} collective-permute-done((bf16[3,48,384]{2,1,0:T(8,128)(2,1)S(1)}, bf16[3,48,384]{2,1,0:T(8,128)(2,1)S(1)}, u32[]{:S(2)}, u32[]{:S(2)}) %collective-permute-start.14) | collective-permute-done | bytes 110624 | tf_op jit(solution)/shard_map/ppermute | solution.py:637
  91.7 4.2 %fold.1 = (bf16[512,384]{1,0:T(8,128)(2,1)S(1)}, f32[512,384]{1,0:T(8,128)}, f32[512,384]{1,0:T(8,128)}, f32[512,384]{1,0:T(8,128)}, bf16[128,384]{1,0:T(8,128)(...) custom-call(s32[4]{0:T(128)S(1)} %get-tuple-element.206.refs_0_, ...), custom_call_target="tpu_custom_call" | custom-call | flops 23000000512 | bytes 5576704 | tf_op jit(solution)/shard_map/fold/pallas_call | solution.py:90
  105.1 7.7 %collective-permute-start.16 = (bf16[128,384]{1,0:T(8,128)(2,1)S(1)}, bf16[128,384]{1,0:T(8,128)(2,1)S(1)}, u32[]{:S(2)}, u32[]{:S(2)}) collective-permute-start(bf16[128,384]{1,0:T(8,128)(2,1)S(1)} %copy-done.26), channel_id=1, source_target_pairs={{0,1},{1,2},{2,3},{3,0},{4,5},{5,6},{6,7},{7,4},{8,9},{9,10},{10,1... | collective-permute-start | bytes 294920 | tf_op jit(solution)/shard_map/ppermute | solution.py:640
  132.8 4.1 %feed.4 = (bf16[256,768]{1,0:T(8,128)(2,1)S(1)}, bf16[256,1536]{1,0:T(8,128)(2,1)S(1)}, f32[256,768]{1,0:T(8,128)S(1)}) custom-call(s32[4]{0:T(128)S(1)} %pad_add_fusion.1.refs_0_, bf16[256,768]{1,0:T(8,128)(2,1)S(1)} %get-tuple-element.132.refs_1_.refs_9_, bf16[256,768]{1,0:T(8,128)(2,1)S(1)} %copy-done.4, ...), custom_call_target="tpu_custom_call" | custom-call | flops 5750000128 | bytes 6291456 | tf_op jit(solution)/shard_map/feed/pallas_call | solution.py:90
  141.2 4.3 %feed.5 = (bf16[256,768]{1,0:T(8,128)(2,1)S(1)}, bf16[256,1536]{1,0:T(8,128)(2,1)S(1)}, bf16[256,768]{1,0:T(8,128)(2,1)S(1)}) custom-call(s32[4]{0:T(128)S(1)} %pad_add_fusion.1.refs_0_, bf16[256,768]{1,0:T(8,128)(2,1)S(1)} %collective-permute-done.23.refs_1_.refs_10_, bf16[256,768]{1,0:T(8,128)(2,1)S(1)} %collective-permute-done.11.refs_11_.refs_2_.refs_14_, ...), custom_call_target="tpu_custom_call" | custom-call | flops 5750000128 | bytes 5898240 | tf_op jit(solution)/shard_map/feed/pallas_call | solution.py:90
  149.1 4.2 %feed.6 = (bf16[256,768]{1,0:T(8,128)(2,1)S(1)}, bf16[256,1536]{1,0:T(8,128)(2,1)S(1)}, bf16[256,768]{1,0:T(8,128)(2,1)S(1)}) custom-call(s32[4]{0:T(128)S(1)} %pad_add_fusion.1.refs_0_, bf16[256,768]{1,0:T(8,128)(2,1)S(1)} %collective-permute-done.24.refs_1_.refs_11_, bf16[256,768]{1,0:T(8,128)(2,1)S(1)} %copy-done.6, ...), custom_call_target="tpu_custom_call" | custom-call | flops 5750000128 | bytes 5898240 | tf_op jit(solution)/shard_map/feed/pallas_call | solution.py:90
  155.2 4.2 %feed.7 = (bf16[256,768]{1,0:T(8,128)(2,1)S(1)}, bf16[256,1536]{1,0:T(8,128)(2,1)S(1)}, bf16[256,768]{1,0:T(8,128)(2,1)S(1)}) custom-call(s32[4]{0:T(128)S(1)} %pad_add_fusion.1.refs_0_, bf16[256,768]{1,0:T(8,128)(2,1)S(1)} %collective-permute-done.25.refs_1_.refs_12_, bf16[256,768]{1,0:T(8,128)(2,1)S(1)} %collective-permute-done.21.refs_9_.refs_2_.refs_16_, ...), custom_call_target="tpu_custom_call" | custom-call | flops 5750000128 | bytes 5898240 | tf_op jit(solution)/shard_map/feed/pallas_call | solution.py:90
  161.7 8.7 %collective-permute-done.27.refs_6_ = bf16[256,768]{1,0:T(8,128)(2,1)S(1)} collective-permute-done((bf16[256,768]{1,0:T(8,128)(2,1)S(1)}, bf16[256,768]{1,0:T(8,128)(2,1)S(1)}, u32[]{:S(2)}, u32[]{:S(2)}) %collective-permute-start.27) | collective-permute-done | bytes 393248 | tf_op jit(solution)/shard_map/ppermute | solution.py:637
  178.8 4.7 %mix_back.1 = (bf16[512,384]{1,0:T(8,128)(2,1)S(1)}, bf16[128,384]{1,0:T(8,128)(2,1)S(1)}, bf16[128,384]{1,0:T(8,128)(2,1)S(1)}, bf16[128,384]{1,0:T(8,128)(2,1)...) custom-call(s32[4]{0:T(128)S(1)} %pad_add_fusion.1.refs_0_, ...), custom_call_target="tpu_custom_call" | custom-call | flops 5750000128 | bytes 6094848 | tf_op jit(solution)/shard_map/mix_back/pallas_call | solution.py:90
  185.1 5.5 %feed_weights.2 = bf16[4,320,768]{2,1,0:T(8,128)(2,1)} custom-call(s32[4]{0:T(128)S(1)} %pad_add_fusion.1.refs_0_, bf16[256,768]{1,0:T(8,128)(2,1)S(1)} %copy-done.51, bf16[256,768]{1,0:T(8,128)(2,1)S(1)} %copy-done.53, bf16[256,768]{1,0:T(8,128)(2,1)S(1)} %copy-done.55, bf16[256,768]{1,0:T(8,128)(2,1)S(1)} %copy-done.57, bf16[256,1536]{1,0:T(8,128)(2,1)} %copy-done.46, ...), custom_call_target="tpu_custom_call" | custom-call | flops 5750000128 | bytes 9830400 | tf_op jit(solution)/shard_map/feed_weights/pallas_call | solution.py:90
  200.9 6.3 %feed_weights.3 = bf16[4,320,768]{2,1,0:T(8,128)(2,1)} custom-call(s32[4]{0:T(128)S(1)} %pad_add_fusion.1.refs_0_, bf16[256,768]{1,0:T(8,128)(2,1)S(1)} %copy-done.51, bf16[256,768]{1,0:T(8,128)(2,1)S(1)} %copy-done.53, bf16[256,768]{1,0:T(8,128)(2,1)S(1)} %copy-done.55, bf16[256,768]{1,0:T(8,128)(2,1)S(1)} %copy-done.57, bf16[256,1536]{1,0:T(8,128)(2,1)} %copy-done.46, ...), custom_call_target="tpu_custom_call" | custom-call | flops 5750000128 | bytes 11796480 | tf_op jit(solution)/shard_map/feed_weights/pallas_call | solution.py:90
  208.6 7.9 %collective-permute-done.35.refs_14_.refs_3_ = bf16[192,768]{1,0:T(8,128)(2,1)} collective-permute-done((bf16[192,768]{1,0:T(8,128)(2,1)}, bf16[192,768]{1,0:T(8,128)(2,1)}, u32[]{:S(2)}, u32[]{:S(2)}) %collective-permute-start.35) | collective-permute-done | bytes 294944 | tf_op jit(solution)/shard_map/ppermute | solution.py:637
  226.9 6.6 %collective-permute-done.38.refs_5_ = bf16[128,384]{1,0:T(8,128)(2,1)S(1)} collective-permute-done((bf16[128,384]{1,0:T(8,128)(2,1)S(1)}, bf16[128,384]{1,0:T(8,128)(2,1)S(1)}, u32[]{:S(2)}, u32[]{:S(2)}) %collective-permute-start.38) | collective-permute-done | bytes 98336 | tf_op jit(solution)/shard_map/ppermute | solution.py:640
  239.9 6.4 %collective-permute-start.44 = (bf16[160,768]{1,0:T(8,128)(2,1)}, bf16[160,768]{1,0:T(8,128)(2,1)S(1)}, u32[]{:S(2)}, u32[]{:S(2)}) collective-permute-start(bf16[160,768]{1,0:T(8,128)(2,1)} %get-tuple-element.181), channel_id=1, source_target_pairs={{0,1},{1,2},{2,3},{3,0},{4,5},{5,6},{6,7},{7,4},{8,9},{9,10},{10,1... | collective-permute-start | bytes 737288 | tf_op jit(solution)/shard_map/ppermute | solution.py:640
  253.6 4.6 %collective-permute-done.44.refs_7_ = bf16[160,768]{1,0:T(8,128)(2,1)S(1)} collective-permute-done((bf16[160,768]{1,0:T(8,128)(2,1)}, bf16[160,768]{1,0:T(8,128)(2,1)S(1)}, u32[]{:S(2)}, u32[]{:S(2)}) %collective-permute-start.44) | collective-permute-done | bytes 245792 | tf_op jit(solution)/shard_map/ppermute | solution.py:640
  261.5 15.8 %reduce-scatter.5.cloned.1.call-done = bf16[1,320,768]{2,1,0:T(8,128)(2,1)} async-done(((bf16[4,320,768]{2,1,0:T(8,128)(2,1)}), bf16[1,320,768]{2,1,0:T(8,128)(2,1)}) %reduce-scatter.5.cloned.1.call-update) | async-done | bytes 491536 | tf_op jit(solution)/shard_map/reduce_scatter | solution.py:899
  284.4 6.0 %collective-permute-start.47 = (bf16[64,768]{1,0:T(8,128)(2,1)S(1)}, bf16[64,768]{1,0:T(8,128)(2,1)S(1)}, u32[]{:S(2)}, u32[]{:S(2)}) collective-permute-start(bf16[64,768]{1,0:T(8,128)(2,1)S(1)} %get-tuple-element.185), channel_id=1, source_target_pairs={{0,1},{1,2},{2,3},{3,0},{4,5},{5,6},{6,7},{7,4},{8,9},{9,10},{10,1... | collective-permute-start | bytes 294920 | tf_op jit(solution)/shard_map/ppermute | solution.py:640
  301.3 6.5 %collective-permute-start.56 = (bf16[96,768]{1,0:T(8,128)(2,1)S(1)}, bf16[96,768]{1,0:T(8,128)(2,1)S(1)}, u32[]{:S(2)}, u32[]{:S(2)}) collective-permute-start(bf16[96,768]{1,0:T(8,128)(2,1)S(1)} %get-tuple-element.190.refs_5_), channel_id=1, source_target_pairs={{0,1},{1,2},{2,3},{3,0},{4,5},{5,6},{6,7},{7,4},{8,9},{9,10},{10,1... | collective-permute-start | bytes 442376 | tf_op jit(solution)/shard_map/ppermute | solution.py:640
  312.6 6.3 %collective-permute-done.54.refs_3_ = bf16[64,768]{1,0:T(8,128)(2,1)S(1)} collective-permute-done((bf16[64,768]{1,0:T(8,128)(2,1)S(1)}, bf16[64,768]{1,0:T(8,128)(2,1)S(1)}, u32[]{:S(2)}, u32[]{:S(2)}) %collective-permute-start.54) | collective-permute-done | bytes 98336 | tf_op jit(solution)/shard_map/ppermute | solution.py:637
  (354 shorter events, 177.1 us)
Async XLA Ops:
  7.2 92.0 %all-gather.6.cloned.1.call-start = ((), (), s32[]{:S(2)}) async-start(), calls=%async_computation.4 | async-start | bytes 2457600 | tf_op jit(solution)/shard_map/all_gather | solution.py:740
  36.3 21.2 %collective-permute-start.6 = (bf16[3,48,1536]{2,1,0:T(8,128)(2,1)S(1)}, bf16[3,48,1536]{2,1,0:T(8,128)(2,1)S(1)}, u32[]{:S(2)}, u32[]{:S(2)}) collective-permute-start(bf16[3,48,1536]{2,1,0:T(8,128)(2,1)S(1)} %get-tuple-element.109.refs_3_), channel_id=1, source_target_pairs={{0,16},{4,20},{8,24},{12,28},{16,0},{20,4},{24,8},{28,12},{1,17},{... | collective-permute-start | bytes 1327112 | tf_op jit(solution)/shard_map/ppermute | solution.py:637
  37.8 19.7 %collective-permute-start.7 = (bf16[3,48,1536]{2,1,0:T(8,128)(2,1)S(1)}, bf16[3,48,1536]{2,1,0:T(8,128)(2,1)}, u32[]{:S(2)}, u32[]{:S(2)}) collective-permute-start(bf16[3,48,1536]{2,1,0:T(8,128)(2,1)S(1)} %get-tuple-element.109.refs_3_), channel_id=1, source_target_pairs={{0,24},{4,28},{8,16},{12,20},{16,8},{20,12},{24,0},{28,4},{1,25},{... | collective-permute-start | bytes 1327112 | tf_op jit(solution)/shard_map/ppermute | solution.py:637
  41.9 206.8 %reduce-scatter.7.cloned.1.call-start = ((), (), s32[]{:S(2)}) async-start(), calls=%async_computation.5 | async-start | bytes 1966080
  65.4 26.3 %collective-permute-start.11 = (bf16[256,768]{1,0:T(8,128)(2,1)S(1)}, bf16[256,768]{1,0:T(8,128)(2,1)S(1)}, u32[]{:S(2)}, u32[]{:S(2)}) collective-permute-start(bf16[256,768]{1,0:T(8,128)(2,1)S(1)} %get-tuple-element.118.refs_1_.refs_2_.refs_13_), channel_id=1, source_target_pairs={{0,8},{4,12},{8,0},{12,4},{16,24},{20,28},{24,16},{28,20},{1,9},{5... | collective-permute-start | bytes 1179656 | tf_op jit(solution)/shard_map/ppermute | solution.py:637
  66.7 24.9 %collective-permute-start.12 = (bf16[256,768]{1,0:T(8,128)(2,1)S(1)}, bf16[256,768]{1,0:T(8,128)(2,1)S(1)}, u32[]{:S(2)}, u32[]{:S(2)}) collective-permute-start(bf16[256,768]{1,0:T(8,128)(2,1)S(1)} %get-tuple-element.118.refs_1_.refs_2_.refs_13_), channel_id=1, source_target_pairs={{0,16},{4,20},{8,24},{12,28},{16,0},{20,4},{24,8},{28,12},{1,17},{... | collective-permute-start | bytes 1179656 | tf_op jit(solution)/shard_map/ppermute | solution.py:637
  103.7 19.5 %collective-permute-start.21 = (bf16[256,768]{1,0:T(8,128)(2,1)S(1)}, bf16[256,768]{1,0:T(8,128)(2,1)S(1)}, u32[]{:S(2)}, u32[]{:S(2)}) collective-permute-start(bf16[256,768]{1,0:T(8,128)(2,1)S(1)} %cot_far.1), channel_id=1, source_target_pairs={{0,24},{4,28},{8,16},{12,20},{16,8},{20,12},{24,0},{28,4},{1,25},{... | collective-permute-start | bytes 1179656 | tf_op jit(solution)/shard_map/ppermute | solution.py:637
  130.0 19.1 %collective-permute-start.24 = (bf16[256,768]{1,0:T(8,128)(2,1)S(1)}, bf16[256,768]{1,0:T(8,128)(2,1)S(1)}, u32[]{:S(2)}, u32[]{:S(2)}) collective-permute-start(bf16[256,768]{1,0:T(8,128)(2,1)S(1)} %get-tuple-element.132.refs_1_.refs_9_), channel_id=1, source_target_pairs={{0,16},{4,20},{8,24},{12,28},{16,0},{20,4},{24,8},{28,12},{1,17},{... | collective-permute-start | bytes 1179656 | tf_op jit(solution)/shard_map/ppermute | solution.py:637
  131.3 23.9 %collective-permute-start.25 = (bf16[256,768]{1,0:T(8,128)(2,1)S(1)}, bf16[256,768]{1,0:T(8,128)(2,1)S(1)}, u32[]{:S(2)}, u32[]{:S(2)}) collective-permute-start(bf16[256,768]{1,0:T(8,128)(2,1)S(1)} %get-tuple-element.132.refs_1_.refs_9_), channel_id=1, source_target_pairs={{0,24},{4,28},{8,16},{12,20},{16,8},{20,12},{24,0},{28,4},{1,25},{... | collective-permute-start | bytes 1179656 | tf_op jit(solution)/shard_map/ppermute | solution.py:637
  177.5 99.8 %reduce-scatter.5.cloned.1.call-start = ((), (), s32[]{:S(2)}) async-start(), calls=%async_computation.2 | async-start | bytes 2457600 | tf_op jit(solution)/shard_map/reduce_scatter | solution.py:899
  198.4 18.1 %collective-permute-start.35 = (bf16[192,768]{1,0:T(8,128)(2,1)}, bf16[192,768]{1,0:T(8,128)(2,1)}, u32[]{:S(2)}, u32[]{:S(2)}) collective-permute-start(bf16[192,768]{1,0:T(8,128)(2,1)} %get-tuple-element.155), channel_id=1, source_target_pairs={{0,16},{4,20},{8,24},{12,28},{16,0},{20,4},{24,8},{28,12},{1,17},{... | collective-permute-start | bytes 884744 | tf_op jit(solution)/shard_map/ppermute | solution.py:637
  199.5 17.1 %collective-permute-start.36 = (bf16[192,768]{1,0:T(8,128)(2,1)}, bf16[192,768]{1,0:T(8,128)(2,1)}, u32[]{:S(2)}, u32[]{:S(2)}) collective-permute-start(bf16[192,768]{1,0:T(8,128)(2,1)} %get-tuple-element.156), channel_id=1, source_target_pairs={{0,24},{4,28},{8,16},{12,20},{16,8},{20,12},{24,0},{28,4},{1,25},{... | collective-permute-start | bytes 884744 | tf_op jit(solution)/shard_map/ppermute | solution.py:637
  207.2 120.4 %all-gather.4.cloned.1.call-start = ((), (), s32[]{:S(2)}) async-start(), calls=%async_computation.3 | async-start | bytes 4423680 | tf_op jit(solution)/shard_map/all_gather | solution.py:959
  239.9 18.3 %collective-permute-start.40 = (bf16[256,768]{1,0:T(8,128)(2,1)S(1)}, bf16[256,768]{1,0:T(8,128)(2,1)S(1)}, u32[]{:S(2)}, u32[]{:S(2)}) collective-permute-start(bf16[256,768]{1,0:T(8,128)(2,1)S(1)} %get-tuple-element.174), channel_id=1, source_target_pairs={{0,4},{4,0},{8,12},{12,8},{16,20},{20,16},{24,28},{28,24},{1,5},{5... | collective-permute-start | bytes 1179656 | tf_op jit(solution)/shard_map/ppermute | solution.py:634
  239.9 18.3 %collective-permute-start.44 = (bf16[160,768]{1,0:T(8,128)(2,1)}, bf16[160,768]{1,0:T(8,128)(2,1)S(1)}, u32[]{:S(2)}, u32[]{:S(2)}) collective-permute-start(bf16[160,768]{1,0:T(8,128)(2,1)} %get-tuple-element.181), channel_id=1, source_target_pairs={{0,1},{1,2},{2,3},{3,0},{4,5},{5,6},{6,7},{7,4},{8,9},{9,10},{10,1... | collective-permute-start | bytes 737288 | tf_op jit(solution)/shard_map/ppermute | solution.py:640
  246.3 31.1 %collective-permute-start.45 = (bf16[160,768]{1,0:T(8,128)(2,1)}, bf16[160,768]{1,0:T(8,128)(2,1)}, u32[]{:S(2)}, u32[]{:S(2)}) collective-permute-start(bf16[160,768]{1,0:T(8,128)(2,1)} %get-tuple-element.182), channel_id=1, source_target_pairs={{0,2},{1,3},{2,0},{3,1},{4,6},{5,7},{6,4},{7,5},{8,10},{9,11},{10,... | collective-permute-start | bytes 737288 | tf_op jit(solution)/shard_map/ppermute | solution.py:640
  246.3 31.1 %collective-permute-start.46 = (bf16[160,768]{1,0:T(8,128)(2,1)}, bf16[160,768]{1,0:T(8,128)(2,1)}, u32[]{:S(2)}, u32[]{:S(2)}) collective-permute-start(bf16[160,768]{1,0:T(8,128)(2,1)} %get-tuple-element.183), channel_id=1, source_target_pairs={{0,3},{1,0},{2,1},{3,2},{4,7},{5,4},{6,5},{7,6},{8,11},{9,8},{10,9... | collective-permute-start | bytes 737288 | tf_op jit(solution)/shard_map/ppermute | solution.py:640
  248.7 28.7 %collective-permute-start.41 = (bf16[192,768]{1,0:T(8,128)(2,1)S(1)}, bf16[192,768]{1,0:T(8,128)(2,1)S(1)}, u32[]{:S(2)}, u32[]{:S(2)}) collective-permute-start(bf16[192,768]{1,0:T(8,128)(2,1)S(1)} %get-tuple-element.177), channel_id=1, source_target_pairs={{0,8},{4,12},{8,0},{12,4},{16,24},{20,28},{24,16},{28,20},{1,9},{5... | collective-permute-start | bytes 884744 | tf_op jit(solution)/shard_map/ppermute | solution.py:637
  258.2 19.2 %collective-permute-start.42 = (bf16[192,768]{1,0:T(8,128)(2,1)S(1)}, bf16[192,768]{1,0:T(8,128)(2,1)S(1)}, u32[]{:S(2)}, u32[]{:S(2)}) collective-permute-start(bf16[192,768]{1,0:T(8,128)(2,1)S(1)} %get-tuple-element.178), channel_id=1, source_target_pairs={{0,16},{4,20},{8,24},{12,28},{16,0},{20,4},{24,8},{28,12},{1,17},{... | collective-permute-start | bytes 884744 | tf_op jit(solution)/shard_map/ppermute | solution.py:637
  258.2 19.2 %collective-permute-start.43 = (bf16[192,768]{1,0:T(8,128)(2,1)S(1)}, bf16[192,768]{1,0:T(8,128)(2,1)S(1)}, u32[]{:S(2)}, u32[]{:S(2)}) collective-permute-start(bf16[192,768]{1,0:T(8,128)(2,1)S(1)} %get-tuple-element.179), channel_id=1, source_target_pairs={{0,24},{4,28},{8,16},{12,20},{16,8},{20,12},{24,0},{28,4},{1,25},{... | collective-permute-start | bytes 884744 | tf_op jit(solution)/shard_map/ppermute | solution.py:637
  280.9 18.6 %collective-permute-start.50 = (bf16[160,768]{1,0:T(8,128)(2,1)S(1)}, bf16[160,768]{1,0:T(8,128)(2,1)S(1)}, u32[]{:S(2)}, u32[]{:S(2)}) collective-permute-start(bf16[160,768]{1,0:T(8,128)(2,1)S(1)} %get-tuple-element.188.refs_5_), channel_id=1, source_target_pairs={{0,8},{4,12},{8,0},{12,4},{16,24},{20,28},{24,16},{28,20},{1,9},{5... | collective-permute-start | bytes 737288 | tf_op jit(solution)/shard_map/ppermute | solution.py:637
  281.6 17.9 %collective-permute-start.51 = (bf16[160,768]{1,0:T(8,128)(2,1)S(1)}, bf16[160,768]{1,0:T(8,128)(2,1)S(1)}, u32[]{:S(2)}, u32[]{:S(2)}) collective-permute-start(bf16[160,768]{1,0:T(8,128)(2,1)S(1)} %get-tuple-element.188.refs_5_), channel_id=1, source_target_pairs={{0,16},{4,20},{8,24},{12,28},{16,0},{20,4},{24,8},{28,12},{1,17},{... | collective-permute-start | bytes 737288 | tf_op jit(solution)/shard_map/ppermute | solution.py:637
  283.0 16.5 %collective-permute-start.52 = (bf16[160,768]{1,0:T(8,128)(2,1)S(1)}, bf16[160,768]{1,0:T(8,128)(2,1)S(1)}, u32[]{:S(2)}, u32[]{:S(2)}) collective-permute-start(bf16[160,768]{1,0:T(8,128)(2,1)S(1)} %get-tuple-element.188.refs_5_), channel_id=1, source_target_pairs={{0,24},{4,28},{8,16},{12,20},{16,8},{20,12},{24,0},{28,4},{1,25},{... | collective-permute-start | bytes 737288 | tf_op jit(solution)/shard_map/ppermute | solution.py:637
  301.3 17.6 %collective-permute-start.56 = (bf16[96,768]{1,0:T(8,128)(2,1)S(1)}, bf16[96,768]{1,0:T(8,128)(2,1)S(1)}, u32[]{:S(2)}, u32[]{:S(2)}) collective-permute-start(bf16[96,768]{1,0:T(8,128)(2,1)S(1)} %get-tuple-element.190.refs_5_), channel_id=1, source_target_pairs={{0,1},{1,2},{2,3},{3,0},{4,5},{5,6},{6,7},{7,4},{8,9},{9,10},{10,1... | collective-permute-start | bytes 442376 | tf_op jit(solution)/shard_map/ppermute | solution.py:640
  (129 other events, 1036.6 us)
Sparse Core Ops, SparseCore 0:
  42.0 55.0 all-gather.5
  177.6 39.6 reduce-scatter.6
  220.2 57.0 reduce-scatter.4
  279.1 48.4 all-gather.3
